TPU v7x, 128 devices: a whole 4x4x4 slice. The times are simulated.
128 devices in a mesh: section: 4 (over x), dp: 32 (over y, z, core).
Axes of the slice: x: 4, y: 4, z: 4, core: 2. Of those that a mesh axis runs over, the one named last changes fastest.
Arguments:
- tokens: bfloat16 [24576, 768], P('dp'), may hold values from -6 to 6
- cotangent: bfloat16 [24576, 768], P('dp'), may hold values from -6 to 6
- lengths: int32 [64, 3], P('dp'), may hold values from 0 to 361, as said below
- proj_in: bfloat16 [4, 768, 5376], P('section', 'dp'), may hold values from -0.21875 to 0.21875
- proj_attn: bfloat16 [4, 768, 768], P('section', 'dp'), may hold values from -1.5 to 1.5
- proj_down: bfloat16 [4, 3072, 768], P('section', 'dp'), may hold values from -0.109375 to 0.109375
- norm_gain: bfloat16 [4, 768], P('section', 'dp'), may hold values from 0.75 to 1.25
- query_gain: bfloat16 [4, 64], P('section', 'dp'), may hold values from 0.75 to 1.25
- key_gain: bfloat16 [4, 64], P('section', 'dp'), may hold values from 0.75 to 1.25
- up_bias: bfloat16 [4, 3072], P('section', 'dp'), may hold values from -2.5 to 2.5
- out_bias: bfloat16 [4, 768], P('section', 'dp'), may hold values from -2.5 to 2.5
Outputs:
- section_outputs: float32 [4, 24576, 768], P('section', 'dp')
- section_grads: float32 [4, 24576, 768], P('section', 'dp')
- grad_proj_in: float32 [4, 768, 5376], P('section', 'dp')
- grad_proj_attn: float32 [4, 768, 768], P('section', 'dp')
- grad_proj_down: float32 [4, 3072, 768], P('section', 'dp')
- grad_norm_gain: float32 [4, 768], P('section', 'dp')
- grad_query_gain: float32 [4, 64], P('section', 'dp')
- grad_key_gain: float32 [4, 64], P('section', 'dp')
- grad_up_bias: float32 [4, 3072], P('section', 'dp')
- grad_out_bias: float32 [4, 768], P('section', 'dp')
Inputs may be any that keep to these rules, and one draw needn't show every extreme that they name: `lengths`: each slot holds one image of 361 tokens, one of 256 tokens, or three of 100 tokens; unused entries are zero. The first slot holds one of 361.
All inputs are finite; a program needn't handle non-finite values.
Results may differ from a plain program's by a relative error of at most 0.035.
Values may be sent and summed in bfloat16 or wider, within the bound.
No kernel may reach another device: no remote copies, remote signals or barrier semaphores. Data moves between devices by JAX's collectives and lax.ppermute only.
A program may use at most 256 MiB of HBM per device.

v0:
```python
from functools import partial
import math

import jax
import jax.numpy as jnp
from jax import lax
from jax.experimental import pallas as pl
from jax.experimental.pallas import tpu as pltpu
from jax.sharding import PartitionSpec as P

BF = jnp.bfloat16
F32 = jnp.float32
VMEM_LIMIT = 56 * 1024 * 1024
SMALL_LIMIT = 30 * 1024 * 1024
EPS = 1e-06
NN = (((1,), (0,)), ((), ()))
NT = (((1,), (1,)), ((), ()))
TN = (((0,), (0,)), ((), ()))
LANES = 128
WIDE = 256
ABSENT = 16
FIRST, LOCAL, ARRIVED = range(3)


def mm(a, b, dims=NN):
    return lax.dot_general(a, b, dims, preferred_element_type=F32)


def head_mean(x, spread, exact):
    parts = []
    for at in range(0, x.shape[1], WIDE):
        piece = x[:, at : at + WIDE]
        top = piece.astype(BF)
        total = mm(top, spread)
        if exact:
            total = total + mm((piece - top.astype(F32)).astype(BF), spread)
        parts.append(total)
    return jnp.concatenate(parts, axis=1)


def row_norm(x):
    centered = x - jnp.mean(x, axis=-1, keepdims=True)
    rstd = lax.rsqrt(jnp.mean(centered * centered, axis=-1, keepdims=True) + EPS)
    return centered * rstd, rstd


def norm_back(grad, normal, rstd, spread):
    return rstd * (grad - head_mean(grad, spread, False) - normal * head_mean(grad * normal, spread, False))


def lane_half(x, second):
    lane = lax.broadcasted_iota(jnp.int32, x.shape, 1)
    return jnp.where((lane >= LANES // 2) if second else (lane < LANES // 2), x, jnp.zeros_like(x))


class Copies:
    def __init__(self, sems):
        self.sems, self.used = sems, 0

    def start(self, src, dst):
        copy = pltpu.make_async_copy(src, dst, self.sems.at[self.used])
        self.used += 1
        copy.start()
        return copy

    def either(self, flag, src, yes, no):
        sem = self.sems.at[self.used]
        self.used += 1

        @pl.when(flag == 1)
        def _():
            pltpu.make_async_copy(src, yes, sem).start()

        @pl.when(flag != 1)
        def _():
            pltpu.make_async_copy(src, no, sem).start()

        return pltpu.make_async_copy(src, yes, sem)


def result_out(home, value, result, rounded, send, copies):
    sem = copies.sems.at[copies.used]
    copies.used += 1

    @pl.when(home == 1)
    def _():
        copy = pltpu.make_async_copy(value, result, sem)
        copy.start()
        copy.wait()

    @pl.when(home != 1)
    def _():
        copy = pltpu.make_async_copy(rounded, send, sem)
        copy.start()
        copy.wait()


def forward_kernel(d, ff, chunks, stride, kind, idx, *refs):
    @pl.when(idx[0] == 1)
    def _():
        forward_work(d, ff, chunks, stride, kind, idx, *refs)


def head_spread(head):
    row = lax.broadcasted_iota(jnp.int32, (WIDE, WIDE), 0) // head
    column = lax.broadcasted_iota(jnp.int32, (WIDE, WIDE), 1) // head
    return jnp.where(row == column, 1.0 / head, 0.0).astype(BF)


def as_column(row):
    return jnp.broadcast_to(row, (LANES, row.shape[1])).T[:, :1]


def forward_work(d, ff, chunks, stride, kind, idx, x_in, g, g3, ids, smalls, *refs):
    refs = refs[13:]
    ybf, xs, qs, ks, vs, ns, nrs, gps, es, small, kept, sent, y_out, y_send = refs[:14]
    (x_v, h_v, w_v, u_v, d_v, a_v, q_v, k_v, v_v, n_v, r_v, act_v, gp_v, e_v, rs_v, att_v, acc_v, y_v, yb_v, id_v, sm_v, ins, outs) = refs[14:]
    rows = x_v.shape[0]
    body_rows = pl.ds(0, rows)
    fc = ff // chunks
    core, slot, home = idx[1], idx[2], idx[3]
    base = jnp.where(home == 1, 0, stride)

    def columns(at, width):
        return pl.ds(pl.multiple_of(base + at, LANES), width)

    cin, cout = Copies(ins), Copies(outs)
    x_copy = None if kind == ARRIVED else cin.start(x_in.at[slot] if kind == FIRST else x_in, x_v)
    small_copies = [cin.start(ids.at[slot], id_v), cin.start(smalls.at[1 - home], sm_v)]
    wq = [cin.start(g.at[:, columns(ff + d * i, d)], w_v.at[:, pl.ds(d * i, d)]) for i in range(3)]
    groups = fc // WIDE
    wff = []
    for c in range(chunks):
        wff.append([cin.start(g.at[:, columns(fc * c, fc)], u_v.at[c])] + [
            cin.start(g3.at[pl.ds(groups * c, groups), :, columns(ff + 4 * d + d * j, d)], d_v.at[pl.ds(groups * c, groups), j])
            for j in range(4)
        ])
    wa = cin.start(g.at[:, columns(ff + 3 * d, d)], a_v)

    pending = []

    def side(i):
        return pl.ds(ff + d * i, d)

    spread = head_spread(64)
    for copy in small_copies:
        copy.wait()
    ids_row = id_v[0:1]
    ids_col = as_column(ids_row)
    keep = jnp.where(ids_col < ABSENT, 1.0, 0.0)
    if kind == ARRIVED:
        x_v[...] = x_in[...]
    else:
        x_copy.wait()
    masked = keep * x_v[...].astype(F32)
    h_v[...] = (row_norm(masked)[0] * sm_v[0:1, :d]).astype(BF)
    pending += [cout.start(x_v, xs), cout.start(h_v, kept.at[body_rows, side(2)]), cout.start(h_v, sent.at[body_rows, side(2)])]
    bias_mask = jnp.where(ids_col == ids_row, 0.0, -1e9)
    for i in range(3):
        wq[i].wait()
        raw = mm(h_v[...], w_v[:, d * i : d * i + d])
        if i == 2:
            v_v[...] = raw.astype(BF)
            pending.append(cout.start(v_v, vs))
        else:
            centered = raw - head_mean(raw, spread, True)
            rstd = lax.rsqrt(head_mean(centered * centered, spread, True) + EPS)
            normal = centered * rstd
            scaled = (normal * sm_v[0:1, d * (2 + i) : d * (3 + i)]).astype(BF)
            n_v[:, d * i : d * i + d] = normal.astype(BF)
            r_v[:, d * i : d * i + d] = rstd.astype(BF)
            if i == 0:
                q_v[...] = scaled * jnp.asarray(0.125, BF)
                pending.append(cout.start(q_v, qs))
            else:
                k_v[...] = scaled
                pending.append(cout.start(k_v, ks))
    pending += [cout.start(n_v, ns), cout.start(r_v, nrs)]
    ones = jnp.ones((16, rows), BF)
    pairs = d // LANES // chunks
    for c in range(chunks):
        for copy in wff[c]:
            copy.wait()
        pre = mm(h_v[...], u_v[c]) + sm_v[1:2, fc * c : fc * c + fc]
        cdf = 0.5 * (1.0 + lax.erf(pre * (1.0 / math.sqrt(2.0))))
        density = jnp.exp(-0.5 * pre * pre) * (1.0 / math.sqrt(2.0 * math.pi))
        act = (pre * cdf).astype(BF)
        act_v[c] = act
        gp_v[c] = (cdf + pre * density).astype(BF)
        total = mm(act, d_v[groups * c : groups * c + groups].reshape(fc, d))
        if c == 0:
            acc_v[...] = total
        else:
            acc_v[...] += total
        for p in range(pairs * c, pairs * c + pairs):
            cols = slice(LANES * p, LANES * p + LANES)
            vals_t = v_v[:, cols].T
            pair = q_v[:, cols]
            both = []
            for half in range(2):
                h = 2 * p + half
                e = jnp.exp(mm(k_v[:, cols], lane_half(pair, half), NT) + bias_mask).astype(BF)
                e_v[h] = e
                got = mm(jnp.concatenate([vals_t[64 * half : 64 * half + 64], ones], axis=0), e)
                inv = 1.0 / got[64:65]
                rs_v[h : h + 1, :] = inv
                both.append((got[:64] * inv).astype(BF))
            att_v[:, cols] = jnp.concatenate(both, axis=0).T
        span = pl.ds(fc * c, fc)
        pending += [cout.either(core, act_v.at[c], sent.at[body_rows, span], kept.at[body_rows, span]), cout.start(gp_v.at[c], gps.at[c]),
                    cout.start(e_v.at[pl.ds(2 * pairs * c, 2 * pairs)], es.at[pl.ds(2 * pairs * c, 2 * pairs)])]
    pending += [cout.start(rs_v, small), cout.either(core, att_v, sent.at[body_rows, side(3)], kept.at[body_rows, side(3)])]
    wa.wait()
    y = keep * (keep * x_v[...].astype(F32) + acc_v[...] + mm(att_v[...], a_v[...]) + sm_v[0:1, d : 2 * d])
    y_v[...] = y
    yb_v[...] = y.astype(BF)
    pending.append(cout.start(yb_v, ybf))
    result_out(home, y_v, y_out.at[slot], yb_v, y_send, cout)
    for copy in pending:
        copy.wait()


def backward_kernel(d, ff, chunks, stride, kind, idx, *refs):
    @pl.when(idx[0] == 1)
    def _():
        backward_work(d, ff, chunks, stride, kind, idx, *refs)


def backward_work(d, ff, chunks, stride, kind, idx, g_in, g, g3, ids, smalls, *refs):
    xs, qs, ks, vs, ns, nrs, gps, es, small = refs[:9]
    refs = refs[9 + 4 :]
    gbf, kept, sent, gr_out, gr_send = refs[:5]
    (g_v, gb_v, w_v, u_v, d_v, a_v, x_v, q_v, k_v, v_v, n_v, r_v, gp_v, e_v, rs_v, gat_v, gqt_v, gk_v,
     gq_b, gk_b, gv_b, gj_v, acc_v, out_v, ob_v, sm_v, sp_v, id_v, gain_v, ins, outs) = refs[5:]
    rows = x_v.shape[0]
    body_rows = pl.ds(0, rows)
    fc = ff // chunks
    groups = fc // WIDE
    core, slot, home = idx[1], idx[2], idx[3]
    base = jnp.where(home == 1, 0, stride)

    def columns(at, width):
        return pl.ds(pl.multiple_of(base + at, LANES), width)

    cin, cout = Copies(ins), Copies(outs)
    g_copy = None if kind == ARRIVED else cin.start(g_in.at[slot] if kind == FIRST else g_in, g_v)
    small_copies = [cin.start(ids.at[slot], id_v), cin.start(smalls.at[1 - home], gain_v)]
    wa = cin.start(g.at[:, columns(ff + 3 * d, d)], a_v)
    heads = [cin.start(s, v) for s, v in ((small, rs_v), (ks, k_v), (vs, v_v), (qs, q_v))]
    pairs = d // LANES // chunks
    wff = []
    for c in range(chunks):
        wff.append(
            [cin.start(g3.at[pl.ds(groups * c, groups), :, columns(ff + 4 * d + d * j, d)], d_v.at[pl.ds(groups * c, groups), j])
             for j in range(4)]
            + [cin.start(gps.at[c], gp_v.at[c]), cin.start(g.at[:, columns(fc * c, fc)], u_v.at[c]),
               cin.start(es.at[pl.ds(2 * pairs * c, 2 * pairs)], e_v.at[pl.ds(2 * pairs * c, 2 * pairs)])]
        )
    norms = [cin.start(ns, n_v), cin.start(nrs, r_v)]
    wq = [cin.start(g.at[:, columns(ff + d * i, d)], w_v.at[:, pl.ds(d * i, d)]) for i in range(3)]
    rows_in = cin.start(xs, x_v)

    pending = []

    def side(i):
        return pl.ds(ff + d * i, d)

    def summed(at, value):
        sm_v[:, at : at + value.shape[1]] = jnp.sum(value, axis=0, keepdims=True)

    spread = head_spread(64)
    for copy in small_copies:
        copy.wait()
    keep = jnp.where(as_column(id_v[0:1]) < ABSENT, 1.0, 0.0)
    if kind == ARRIVED:
        g_v[...] = g_in[...]
    else:
        g_copy.wait()
    gres = keep * g_v[...].astype(F32)
    summed(d, gres)
    gb_v[...] = gres.astype(BF)
    pending.append(cout.either(core, gb_v, sent.at[body_rows, side(0)], kept.at[body_rows, side(0)]))
    wa.wait()
    gat_v[...] = mm(a_v[...], gb_v[...], NT).astype(BF)
    for copy in heads:
        copy.wait()
    zeros = jnp.zeros((LANES // 2, rows), BF)
    for c in range(chunks):
        for copy in wff[c]:
            copy.wait()
        gup = mm(gb_v[...], d_v[groups * c : groups * c + groups].reshape(fc, d), NT) * gp_v[c].astype(F32)
        summed(4 * d + fc * c, gup)
        gup = gup.astype(BF)
        gj_v[c] = gup
        span = pl.ds(fc * c, fc)
        pending.append(cout.either(core, gj_v.at[c], kept.at[body_rows, span], sent.at[body_rows, span]))
        total = mm(gup, u_v[c], NT)
        if c == 0:
            acc_v[...] = total
        else:
            acc_v[...] += total
        for p in range(pairs * c, pairs * c + pairs):
            cols = slice(LANES * p, LANES * p + LANES)
            keys, vals, pair = k_v[:, cols], v_v[:, cols], q_v[:, cols]
            keys_t = keys.T
            gk, gv = None, None
            for half in range(2):
                h = 2 * p + half
                at_rows = slice(64 * h, 64 * h + 64)
                inv = rs_v[h : h + 1, :]
                ga = (gat_v[at_rows, :].astype(F32) * inv).astype(BF)
                ga = jnp.concatenate([zeros, ga] if half else [ga, zeros], axis=0)
                e = e_v[h]
                ef = e.astype(F32)
                gp = ef * mm(vals, ga)
                dot = jnp.sum(gp, axis=0, keepdims=True) * inv
                gs = (gp - ef * dot).astype(BF)
                gk_h = mm(gs, lane_half(pair, half))
                gv_h = mm(e, ga, NT)
                gk = gk_h if gk is None else gk + gk_h
                gv = gv_h if gv is None else gv + gv_h
                gqt_v[at_rows, :] = mm(keys_t[64 * half : 64 * half + 64], gs) * 0.125
            gk_v[:, cols] = gk
            gv_b[:, cols] = gv.astype(BF)
    pending.append(cout.either(core, gv_b, sent.at[body_rows, side(1)], kept.at[body_rows, side(1)]))
    for copy in norms:
        copy.wait()
    for i, (grad, out) in enumerate(((gqt_v[...].T, gq_b), (gk_v[...], gk_b))):
        normal = n_v[:, d * i : d * i + d].astype(F32)
        summed(2 * d + d * i, grad * normal)
        gain = gain_v[0:1, d * (2 + i) : d * (3 + i)]
        out[...] = norm_back(grad * gain, normal, r_v[:, d * i : d * i + d].astype(F32), spread).astype(BF)
        pending.append(cout.either(core, out, kept.at[body_rows, side(i)], sent.at[body_rows, side(i)]))
    for copy in wq:
        copy.wait()
    ghid = acc_v[...]
    for i, part in enumerate((gq_b, gk_b, gv_b)):
        ghid = ghid + mm(part[...], w_v[:, d * i : d * i + d], NT)
    rows_in.wait()
    xhat, rstd = row_norm(keep * x_v[...].astype(F32))
    summed(0, ghid * xhat)
    top = sm_v[...].astype(BF).astype(F32)
    sp_v[...] = jnp.concatenate([top, sm_v[...] - top, jnp.zeros((14, top.shape[1]), F32)], axis=0).astype(BF)
    tail = pl.ds(rows, 16)
    pending += [cout.start(sp_v, kept.at[tail]), cout.start(sp_v, sent.at[tail])]
    gx = ghid * gain_v[0:1, :d]
    gmask = rstd * (gx - jnp.mean(gx, axis=-1, keepdims=True) - xhat * jnp.mean(gx * xhat, axis=-1, keepdims=True))
    out = keep * (keep * g_v[...].astype(F32) + gmask)
    out_v[...] = out
    ob_v[...] = out.astype(BF)
    pending.append(cout.start(ob_v, gbf))
    result_out(home, out_v, gr_out.at[slot], ob_v, gr_send, cout)
    for copy in pending:
        copy.wait()


def split_small(values):
    top = values.astype(BF).astype(F32)
    lane = lax.broadcasted_iota(jnp.int32, values.shape, 1)
    return jnp.where(lane < 8, top, jnp.where(lane < 16, pltpu.roll(values - top, 8, 1), 0.0)).astype(BF)


def joined_small(parts):
    return parts + pltpu.roll(parts, LANES - 8, 1)


def small_table(d, ff, tables):
    total = jnp.zeros((1, tables.shape[2]), F32)
    for i in range(tables.shape[0]):
        parts = tables[i].astype(F32)
        total = total + parts[0:1] + parts[1:2]
    lane = lax.broadcasted_iota(jnp.int32, (LANES, d), 0) % 64
    place = jnp.where(lax.broadcasted_iota(jnp.int32, (LANES, d), 1) == lane // 2 * 24 + lane % 2, 1.0, 0.0)
    quarter = WIDE // 4
    ub = total[:, 4 * d :]
    up_rows = []
    for j in range(4):
        pieces = [ub[:, WIDE * b + quarter * j : WIDE * b + quarter * (j + 1)] for b in range(ff // WIDE)]
        up_rows.append(jnp.concatenate(pieces, axis=1))
    head_rows = []
    for i in range(2, 4):
        lanes = total[:, d * i : d * i + LANES]
        for p in range(1, d // LANES):
            lanes = lanes + total[:, d * i + LANES * p : d * i + LANES * (p + 1)]
        head_rows.append(lanes)
    both = jnp.concatenate(head_rows + [jnp.zeros((6, LANES), F32)], axis=0)
    placed = lax.dot_general(both, place, NN, precision=lax.Precision.HIGHEST, preferred_element_type=F32)
    rows = [total[:, :d], total[:, d : 2 * d]] + up_rows + [placed[0:1], placed[1:2], jnp.zeros((LANES - 8, d), F32)]
    return jnp.concatenate(rows, axis=0).T


def weight_grad_kernel(d, ff, idx, kept, got, *refs):
    results, (big_v, a_v, b_v, c_v, out_v, t_v, ins, outs) = refs[:5], refs[5:]
    rows = kept.shape[0] - t_v.shape[1]
    tokens = 2 * rows
    quarter, half, third = WIDE // 4, ff // 2, ff // 3
    blocks = third // WIDE
    share = d // 16
    cut = 3 * d
    y, z, core = idx[0], idx[1], idx[2]

    def load(cin, at, width, to, to_at):
        return [cin.start(src.at[pl.ds(0, rows), pl.ds(at, width)], to.at[i, :, pl.ds(to_at, width)]) for i, src in enumerate((kept, got))]

    def wait(copies):
        for copy in copies:
            copy.wait()

    def both(ref, at=0, width=d):
        return ref[:, :, at : at + width].reshape(tokens, width)

    def put(rows_at, cols_at, value):
        out_v[rows_at, cols_at] = value.astype(BF)

    def send_by_y(cout, at, width):
        cols = pl.ds(at, width)

        def rows_of(s, first, count):
            return out_v.at[pl.ds(pl.multiple_of(lax.rem(y + s, 4) * 4 * share + first, 16), count), cols]

        return [cout.start(rows_of(2, 0, 2 * share), results[3].at[:, cols]),
                cout.start(rows_of(2, 2 * share, 2 * share), results[4].at[:, cols])] + [
            cout.start(rows_of(s, 0, 4 * share), results[r].at[:, cols]) for r, s in ((1, 1), (2, 3), (0, 0))]

    def send_by_z(cout, at, width):
        cols = pl.ds(at, width)

        def rows_of(i, s):
            return out_v.at[pl.ds(pl.multiple_of((4 * i + lax.rem(z + s, 4)) * share, 16), share), cols]

        return [
            cout.start(rows_of(i, s), results[r].at[pl.ds(share * (i - base), share), cols])
            for r, s, base, count in ((3, 2, 0, 2), (4, 2, 2, 2), (1, 1, 0, 4), (2, 3, 0, 4), (0, 0, 0, 4))
            for i in range(base, base + count)
        ]

    everything = slice(0, d)

    @pl.when(core == 0)
    def _():
        cin, cout = Copies(ins), Copies(outs)
        grads = load(cin, ff, d, a_v, 0)
        loads = [load(cin, third * k, third, big_v, third * k) for k in range(3)]
        attended = load(cin, ff + 3 * d, d, b_v, 0)
        hidden, values = load(cin, ff + 2 * d, d, c_v, 0), load(cin, ff + d, d, c_v, d)
        smalls = [cin.start(src.at[pl.ds(rows, t_v.shape[1])], t_v.at[i]) for i, src in enumerate((kept, got))]
        wait(grads)
        gb = both(a_v)
        for k in range(3):
            wait(loads[k])
            found = lax.dot_general(both(big_v, third * k, third), gb, TN, preferred_element_type=F32).astype(BF)
            for b in range(blocks):
                at = quarter * (blocks * k + b)
                for j in range(4):
                    put(slice(at, at + quarter), slice(d * j, d * j + d), found[WIDE * b + quarter * j : WIDE * b + quarter * (j + 1)])
        pending = send_by_y(cout, 0, 4 * d)
        wait(attended)
        put(everything, slice(4 * d, 5 * d), lax.dot_general(both(b_v), gb, TN, preferred_element_type=F32))
        wait(hidden + values + smalls)
        put(everything, slice(5 * d, 6 * d), lax.dot_general(both(c_v), both(c_v, d), TN, preferred_element_type=F32))
        put(everything, slice(6 * d, 6 * d + LANES), split_small(small_table(d, ff, t_v)))
        wait(pending + send_by_y(cout, 4 * d, 2 * d + LANES))

    @pl.when(core == 1)
    def _():
        cin, cout = Copies(ins), Copies(outs)
        hidden = load(cin, ff + 2 * d, d, a_v, 0)
        loads = [load(cin, third * k, third, big_v, third * k) for k in range(2)]
        queries = load(cin, ff, d, b_v, 0)
        loads.append(load(cin, 2 * third, third, big_v, 2 * third))
        keys = load(cin, ff + d, d, c_v, 0)
        wait(hidden)
        turned = both(a_v).T
        pending = []
        for k in range(2):
            wait(loads[k])
            put(everything, slice(third * k, third * k + third), mm(turned, both(big_v, third * k, third)))
        pending = send_by_z(cout, 0, 2 * third)
        wait(queries)
        put(everything, slice(ff, ff + d), mm(turned, both(b_v)))
        wait(loads[2])
        put(everything, slice(2 * third, ff), mm(turned, both(big_v, 2 * third, third)))
        wait(keys)
        put(everything, slice(ff + d, ff + 2 * d), mm(turned, both(c_v)))
        out_v[:, 6 * d :] = jnp.zeros((d, LANES), BF)
        wait(pending + send_by_z(cout, 2 * third, 6 * d + LANES - 2 * third))


def added(parts):
    total = parts[0][...].astype(F32)
    for part in parts[1:]:
        total = total + part[...].astype(F32)
    shape = total.shape
    total = total.reshape(-1, shape[-1])
    main, last = total[:, : shape[-1] - LANES], split_small(joined_small(total[:, shape[-1] - LANES :]))
    return jnp.concatenate([main.astype(BF), last], axis=1).reshape(shape)


def relay_kernel(idx, up_in, down_in, up_got, down_got, up, down, hold, ins, outs):
    half = up_got.shape[0]
    cin, cout = Copies(ins), Copies(outs)
    parts = ((up_in, 0, up_got, up), (down_in, half, down_got, down))
    loads = [cin.start(block.at[pl.ds(at, half)], hold.at[i]) for i, (block, at, _, _) in enumerate(parts)]
    pending = []
    for i, (_, at, got, out) in enumerate(parts):
        loads[i].wait()
        hold[i] = added([hold.at[i], got])
        pending.append(cout.start(hold.at[i], out.at[pl.ds(at, half)]))
    for copy in pending:
        copy.wait()


def mid_kernel(idx, *refs):
    came, results, (in_v, out_v, ins, outs) = refs[:3], refs[3:7], refs[7:]
    share = results[0].shape[0]

    cin, cout = Copies(ins), Copies(outs)
    at = jnp.where(idx[2] == 0, idx[1], idx[0])
    order = [2, 1, 3, 0]
    blocks = [pl.multiple_of(lax.rem(at + s, 4) * share, 16) for s in order]
    loads = [[cin.start(part.at[pl.ds(block, share)], in_v.at[i, p]) for p, part in enumerate(came)]
             for i, block in enumerate(blocks)]
    pending = []
    for i, s in enumerate(order):
        for copy in loads[i]:
            copy.wait()
        out_v[i] = added([in_v.at[i, p] for p in range(3)])
        pending.append(cout.start(out_v.at[i], results[s]))
    for copy in pending:
        copy.wait()


def last_pair_kernel(idx, *refs):
    came, (home_mine, home_other, away_mine, away_other, in_v, hold, ins) = refs[:8], refs[8:]
    share = home_mine.shape[0]
    core, odd = idx[2], idx[4]

    sum_of(came, in_v, hold, ins)

    def rows_of(k, which):
        return hold[k, pl.ds(pl.multiple_of(which * share, 8), share), :]

    for which, home, away in ((core, home_mine, away_mine), (1 - core, home_other, away_other)):
        home[...] = jnp.where(odd == 1, rows_of(1, which), rows_of(0, which)).astype(home.dtype)
        away[...] = jnp.where(odd == 1, rows_of(0, which), rows_of(1, which)).astype(away.dtype)


def sum_of(came, in_v, hold, sems):
    copies = Copies(sems)
    loads = [copies.start(came[4 * k], in_v.at[k]) for k in range(len(came) // 4)]
    for k, load in enumerate(loads):
        load.wait()
        hold[k] = added([in_v.at[k]] + list(came[4 * k + 1 : 4 * k + 4])).astype(F32)


def place_kernel(idx, y_in, y_got, g_in, g_got, y_out, g_out, y_v, g_v, sems):
    copies = Copies(sems)
    pending = []
    for got, wide_v, out in ((y_got, y_v, y_out), (g_got, g_v, g_out)):
        wide_v[...] = got[...].astype(F32)
        pending.append(copies.start(wide_v, out.at[1 - idx[3]]))
    for copy in pending:
        copy.wait()


def picked(rows, columns, wanted):
    row = lax.broadcasted_iota(jnp.int32, (rows, columns), 0)
    column = lax.broadcasted_iota(jnp.int32, (rows, columns), 1)
    return row, column, jnp.where(column == wanted(row), 1.0, 0.0)


def prepare_kernel(d, ff, p_in, p_attn, p_down, n_gain, o_bias, u_bias, q_gain, k_gain, shuffle, out):
    share = p_in.shape[0]
    heads_part = p_in.shape[1] - ff
    for at in range(0, ff, WIDE):
        out[:, at : at + WIDE] = mm(p_in[:, heads_part + at : heads_part + at + WIDE], shuffle[...]).astype(BF)
    out[:, ff : ff + heads_part] = p_in[:, :heads_part]
    at = ff + heads_part
    out[:, at : at + d] = p_attn[...]
    down = p_down[...]
    for j in range(4):
        take = picked(share, down.shape[0], lambda row: 4 * row + j)[2].astype(BF)
        out[:, at + d * (j + 1) : at + d * (j + 2)] = mm(take, down).astype(BF)

    def column_of(ref, wanted, where):
        values = ref[...].astype(F32)
        take = picked(share, values.shape[1], wanted)[2]
        lane = lax.broadcasted_iota(jnp.int32, (share, LANES), 1)
        return jnp.where(lane == where, jnp.sum(take * values, axis=1, keepdims=True), 0.0)

    table = column_of(n_gain, lambda row: row, 0) + column_of(o_bias, lambda row: row, 1)
    for j in range(4):
        table = table + column_of(u_bias, lambda row: 4 * row + j, 2 + j)
    table = table + column_of(q_gain, lambda row: row, 6) + column_of(k_gain, lambda row: row, 7)
    out[:, at + 5 * d :] = table.astype(BF)


def smalls_kernel(d, ff, shares, place, out):
    quarter = WIDE // 4
    for layer in range(2):
        table = shares[:, LANES * layer : LANES * (layer + 1)].astype(F32).T
        pieces = [table[2 + j : 3 + j, quarter * b : quarter * (b + 1)] for b in range(ff // WIDE) for j in range(4)]
        both = mm(table[0:8].astype(BF), place[...])
        first = jnp.concatenate([table[0:1], table[1:2], both[6:7], both[7:8]], axis=1)
        out[layer] = jnp.concatenate([first, jnp.concatenate(pieces, axis=1), jnp.zeros((6, ff), F32)], axis=0)


def in_parts(x):
    top = x.astype(BF)
    rest = x - top.astype(F32)
    middle = rest.astype(BF)
    return top, middle, (rest - middle.astype(F32)).astype(BF)


def finish_kernel(d, ff, idx, own, a_in, b_in, c_in, shuffle, g_in, g_attn, g_down, g_ng, g_q, g_k, g_ub, g_ob):
    core = idx[2]
    share = own.shape[0]
    mine = own[...] + a_in[...].astype(F32)
    theirs = b_in[...].astype(F32) + c_in[...].astype(F32)
    half0 = jnp.where(core == 0, mine, theirs)
    half1 = jnp.where(core == 0, theirs, mine)
    g_in[:, : 2 * d] = half1[:, ff : ff + 2 * d]
    g_in[:, 2 * d : 3 * d] = half0[:, 5 * d : 6 * d]
    for at in range(0, ff, WIDE):
        g_in[:, 3 * d + at : 3 * d + at + WIDE] = sum(mm(part, shuffle[...], NT) for part in in_parts(half1[:, at : at + WIDE]))
    g_attn[...] = half0[:, 4 * d : 5 * d]
    stacked = jnp.concatenate([half0[:, at : at + d] for at in range(0, 4 * d, d)], axis=0)
    row, column, _ = picked(4 * share, 4 * share, lambda row: row)
    turn = jnp.where(column == lax.rem(row, 4) * share + row // 4, 1.0, 0.0).astype(BF)
    g_down[...] = sum(mm(turn, part) for part in in_parts(stacked))
    small = joined_small(half0[:, 6 * d :])
    turned = jnp.concatenate([small, jnp.zeros((LANES - share, LANES), F32)], axis=0).T
    g_ng[...] = turned[0:1, :share]
    g_ob[...] = turned[1:2, :share]
    g_q[...] = turned[6:7, : g_q.shape[1]]
    g_k[...] = turned[7:8, : g_k.shape[1]]
    total = jnp.zeros((8, 4 * share), F32)
    for j in range(4):
        row, column, _ = picked(LANES, 4 * share, lambda row: row)
        spread_out = jnp.where(column == 4 * row + j, 1.0, 0.0)
        total = total + jnp.where(lax.broadcasted_iota(jnp.int32, (8, 4 * share), 0) == 2 + j, 1.0, 0.0) * lax.dot_general(
            turned[0:8], spread_out, NN, precision=lax.Precision.HIGHEST, preferred_element_type=F32)
    g_ub[...] = jnp.sum(total, axis=0, keepdims=True)


ANY = pl.BlockSpec(memory_space=pl.ANY)
HERE = pl.BlockSpec(memory_space=pltpu.VMEM)


def whole(shape):
    return pl.BlockSpec(shape, lambda i, idx: (0,) * len(shape))


def pick(shape):
    return pl.BlockSpec((1,) + shape, lambda i, idx: (idx[2],) + (0,) * len(shape))


def call(kernel, idx, ins, fresh, stashes, scratch, flops):
    outs = pl.pallas_call(
        kernel,
        grid_spec=pltpu.PrefetchScalarGridSpec(
            num_scalar_prefetch=1,
            grid=(1,),
            in_specs=[s for _, s in ins] + [ANY] * len(stashes),
            out_specs=[ANY] * (1 + len(stashes)),
            scratch_shapes=scratch,
        ),
        out_shape=[jax.ShapeDtypeStruct(*fresh)] + [jax.ShapeDtypeStruct(a.shape, a.dtype) for a in stashes],
        input_output_aliases={1 + len(ins) + i: 1 + i for i in range(len(stashes))},
        compiler_params=pltpu.CompilerParams(dimension_semantics=("arbitrary",), vmem_limit_bytes=VMEM_LIMIT),
        cost_estimate=pl.CostEstimate(flops=flops, bytes_accessed=1 << 10, transcendentals=0),
    )(idx, *[a for a, _ in ins], *stashes)
    return outs[0], list(outs[1:])


def plain(kernel, arrays, specs, out_shapes, out_specs, scratch):
    return pl.pallas_call(
        kernel, grid=(1,), in_specs=specs, out_specs=out_specs, scratch_shapes=scratch, out_shape=out_shapes,
        compiler_params=pltpu.CompilerParams(dimension_semantics=("arbitrary",), vmem_limit_bytes=VMEM_LIMIT),
        cost_estimate=pl.CostEstimate(flops=1 << 10, bytes_accessed=1 << 10, transcendentals=0),
    )(*arrays)


def simple(kernel, idx, arrays, specs, out_shapes, out_specs, scratch, limit=VMEM_LIMIT):
    return pl.pallas_call(
        kernel,
        grid_spec=pltpu.PrefetchScalarGridSpec(
            num_scalar_prefetch=1, grid=(1,), in_specs=specs, out_specs=out_specs, scratch_shapes=scratch
        ),
        out_shape=out_shapes,
        compiler_params=pltpu.CompilerParams(dimension_semantics=("arbitrary",), vmem_limit_bytes=limit),
        cost_estimate=pl.CostEstimate(flops=1 << 10, bytes_accessed=1 << 10, transcendentals=0),
    )(idx, *arrays)


def along(x, step, size, by):
    devices = lax.axis_size("dp")

    def to(i):
        digit = i // step % size
        return i + ((digit + by) % size - digit) * step

    return lax.ppermute(x, "dp", [(i, to(i)) for i in range(devices)])


def paired(x):
    return lax.ppermute(x, "section", [(0, 1), (1, 0), (2, 3), (3, 2)])


def body(tokens, cotangent, lengths, proj_in, proj_attn, proj_down, norm_gain, query_gain, key_gain, up_bias, out_bias):
    ranks = lax.axis_size("dp")
    section = lax.axis_index("section")
    rank = lax.axis_index("dp")
    slots = lengths.shape[0]
    rows = tokens.shape[0] // slots
    d = tokens.shape[1]
    joined = proj_in.shape[2]
    ff = proj_down.shape[1] * ranks
    head = query_gain.shape[1] * ranks
    heads = d // head
    dshare = proj_in.shape[1]
    fshare = proj_down.shape[1] // dshare
    hshare = query_gain.shape[1]
    chunks = 3
    wide = joined + d + ff
    stride = wide + LANES
    side = math.isqrt(ranks // 2)
    core, z, y = lax.rem(rank, 2), lax.rem(rank // 2, side), rank // (2 * side)
    stage, odd = section // 2, lax.rem(section, 2)
    slot = lax.rem(stage + odd, 2)

    place = jnp.arange(WIDE, dtype=jnp.int32)
    source = (place % (WIDE // fshare)) * fshare + place // (WIDE // fshare)
    shuffle = (place[:, None] == source[None, :]).astype(BF)

    def full(a):
        return pl.BlockSpec(a.shape, lambda i: (0,) * a.ndim)

    shares = [proj_in[0], proj_attn[0], proj_down[0], norm_gain, out_bias, up_bias, query_gain, key_gain, shuffle]
    heads_part = joined - ff
    local = jax.ShapeDtypeStruct((dshare, stride), BF)
    local = plain(partial(prepare_kernel, d, ff), shares, [full(a) for a in shares], local, full(local), [])
    other = paired(local)
    g = lax.all_gather(jnp.concatenate([local, other], axis=1), "dp", axis=0).reshape(d, 2 * stride)
    shares = jnp.concatenate([local[:, wide:], other[:, wide:]], axis=1)
    step = 1
    while step < ranks:
        got = lax.ppermute(shares, "dp", [(i, i ^ step) for i in range(ranks)])
        low = lax.rem(rank // step, 2) == 0
        shares = jnp.where(low, jnp.concatenate([shares, got]), jnp.concatenate([got, shares]))
        step *= 2
    toks = tokens.reshape(slots, rows, d)
    seeds = cotangent.reshape(slots, rows, d)
    ends = jnp.cumsum(lengths, axis=-1)
    position = jnp.arange(rows, dtype=jnp.int32)
    image = jnp.sum((position[None, :, None] >= ends[:, None, :]).astype(jnp.int32), axis=-1)
    image = jnp.where(position[None, :] < ends[:, 2:3], image, ABSENT + position[None, :])
    ids = jnp.broadcast_to(image[:, None, :].astype(F32), (slots, 8, rows))

    def index_of(layer, active_stage):
        return jnp.stack([stage == active_stage, core, slot, odd == layer]).astype(jnp.int32)

    indices = [[index_of(layer, active) for active in range(2)] for layer in range(2)]
    here = jnp.stack([y, z, core, slot, odd]).astype(jnp.int32)
    element = jnp.arange(d, dtype=jnp.int32) % head
    spread_gain = (jnp.arange(d, dtype=jnp.int32)[:, None] == (element // hshare * dshare + element % hshare)[None, :]).astype(BF)
    small = jax.ShapeDtypeStruct((2, 8, ff), F32)
    smalls = plain(
        partial(smalls_kernel, d, ff), [shares, spread_gain], [full(shares), full(spread_gain)], small, full(small), [],
    )
    g, indices, here, ids, smalls = lax.optimization_barrier((g, indices, here, ids, smalls))
    g3 = g.reshape(ff // WIDE, WIDE // fshare, g.shape[1])
    def stash(*shape, dtype=BF):
        return pl.pallas_call(
            lambda out: None, out_shape=jax.ShapeDtypeStruct(shape, dtype), out_specs=pl.BlockSpec(memory_space=pl.ANY)
        )()

    fc = ff // chunks
    groups = ff // WIDE

    V = pltpu.VMEM
    weights_v = [V((d, heads_part), BF), V((chunks, d, fc), BF), V((groups, fshare, WIDE // fshare, d), BF), V((d, d), BF)]
    sems = [pltpu.SemaphoreType.DMA((48,)), pltpu.SemaphoreType.DMA((48,))]
    stacked = ff + 4 * d
    operands = [[stash(rows + 16, stacked), stash(rows + 16, stacked)] for _ in range(2)]
    kept = [[stash(rows, d) for _ in range(4)] + [stash(rows, 2 * d), stash(rows, 2 * d), stash(chunks, rows, fc),
             stash(heads, rows, rows), stash(16, rows, dtype=F32)] for _ in range(2)]
    results = [stash(slots, rows, d, dtype=F32), stash(rows, d)]
    here_x = toks
    for t in range(4):
        layer = t % 2
        ybf, done = call(
            partial(forward_kernel, d, ff, chunks, stride, (FIRST, LOCAL, ARRIVED, LOCAL)[t]),
            indices[layer][t // 2],
            [(here_x, HERE if t == 2 else ANY)] + [(a, ANY) for a in (g, g3, ids, smalls)],
            ((rows, d), BF),
            kept[layer][:9] + operands[layer] + results,
            [V((rows, d), BF), V((rows, d), BF)] + weights_v
            + [V((rows, d), BF)] * 3 + [V((rows, 2 * d), BF)] * 2 + [V((chunks, rows, fc), BF)] * 2
            + [V((heads, rows, rows), BF), V((16, rows), F32), V((rows, d), BF), V((rows, d), F32), V((rows, d), F32), V((rows, d), BF), V((8, rows), F32), V((8, ff), F32)]
            + sems,
            1 << 10,
        )
        kept[layer], operands[layer], results = done[:9], done[9:11], done[11:]
        here_x = lax.ppermute(ybf, "section", [(0, 3), (1, 2)]) if t == 1 else ybf
    y_out, y_send = results
    y_got = paired(y_send)

    results = [stash(slots, rows, d, dtype=F32), stash(rows, d)]
    width = 6 * d + LANES
    share = 2 * dshare

    def moved(x, leg, by):
        def to(i):
            step = 2 * side if i % 2 == leg else 2
            digit = i // step % side
            return i + ((digit + by) % side - digit) * step

        return lax.ppermute(x, "dp", [(i, to(i)) for i in range(ranks)])

    def grads_by_place(layer, got):
        return simple(
            partial(weight_grad_kernel, d, ff), here,
            [operands[layer][0], got], [ANY] * 2,
            [jax.ShapeDtypeStruct((side * share, width), BF)] * 3 + [jax.ShapeDtypeStruct((side // 2 * share, width), BF)] * 2,
            [ANY] * 5,
            [V((2, rows, ff), BF), V((2, rows, d), BF), V((2, rows, d), BF), V((2, rows, 2 * d), BF), V((d, width), BF), V((2, 16, stacked), BF),
             pltpu.SemaphoreType.DMA((32,)), pltpu.SemaphoreType.DMA((32,))],
        )

    def halves(made):
        return moved(made[3], 0, 1), moved(made[4], 0, -1)

    def first_leg(made, came):
        own, up, down = made[:3]
        part = (side // 2 * share, width)
        up, down = pl.pallas_call(
            relay_kernel,
            grid_spec=pltpu.PrefetchScalarGridSpec(
                num_scalar_prefetch=1, grid=(1,), in_specs=[ANY, ANY, HERE, HERE], out_specs=[ANY] * 2,
                scratch_shapes=[V((2,) + part, BF), pltpu.SemaphoreType.DMA((2,)), pltpu.SemaphoreType.DMA((2,))],
            ),
            out_shape=[jax.ShapeDtypeStruct(up.shape, BF)] * 2,
            input_output_aliases={1: 0, 2: 1},
            compiler_params=pltpu.CompilerParams(dimension_semantics=("arbitrary",), vmem_limit_bytes=SMALL_LIMIT),
            cost_estimate=pl.CostEstimate(flops=1 << 10, bytes_accessed=1 << 10, transcendentals=0),
        )(here, up, down, *came)
        return [own, moved(up, 0, 1), moved(down, 0, -1)]

    def second_leg(outs):
        far, near, back = (moved(outs[s], 1, s) for s in (2, 1, 3))
        return [outs[0], near, far, back]

    def by_second_axis(came):
        return simple(
            mid_kernel, here, came, [ANY] * 3, [jax.ShapeDtypeStruct((share, width), BF)] * side, [ANY] * side,
            [V((side, 3, share, width), BF), V((side, share, width), BF), pltpu.SemaphoreType.DMA((12,)), pltpu.SemaphoreType.DMA((4,))],
        )

    here_g = seeds
    swaps = []
    for t in range(4):
        layer = 1 - t % 2
        gbf, done = call(
            partial(backward_kernel, d, ff, chunks, stride, (FIRST, LOCAL, ARRIVED, LOCAL)[t]),
            indices[layer][1 - t // 2],
            [(here_g, HERE if t == 2 else ANY)] + [(a, ANY) for a in [g, g3, ids, smalls] + kept[layer]],
            ((rows, d), BF),
            operands[layer] + results,
            [V((rows, d), BF), V((rows, d), BF)] + weights_v
            + [V((rows, d), BF)] * 4 + [V((rows, 2 * d), BF)] * 2
            + [V((chunks, rows, fc), BF), V((heads, rows, rows), BF), V((16, rows), F32)]
            + [V((d, rows), BF), V((d, rows), F32), V((rows, d), F32)]
            + [V((rows, d), BF)] * 3 + [V((chunks, rows, fc), BF), V((rows, d), F32), V((rows, d), F32), V((rows, d), BF), V((1, stacked), F32), V((16, stacked), BF), V((8, rows), F32), V((8, ff), F32)]
            + sems,
            1 << 10,
        )
        operands[layer], results = done[:2], done[2:]
        here_g = lax.ppermute(gbf, "section", [(3, 0), (2, 1)]) if t == 1 else gbf
        if t == 1:
            here_g, y_got = lax.optimization_barrier((here_g, y_got))
        if t == 3:
            operands[layer][1], swaps[0] = lax.optimization_barrier((operands[layer][1], swaps[0]))
        if t >= 2:
            swaps.append(along(operands[layer][1], 1, 2, 1))
    gr_got = paired(results[1])
    upper, gr_got = lax.optimization_barrier((grads_by_place(1, swaps[0]), gr_got))
    upper_came = halves(upper)
    lower = grads_by_place(0, swaps[1])
    lower_came = halves(lower)
    legs = [first_leg(upper, upper_came), first_leg(lower, lower_came)]
    arrived = [second_leg(by_second_axis(came)) for came in legs]
    gr_out = results[0]
    y_out, gr_out = pl.pallas_call(
        place_kernel,
        grid_spec=pltpu.PrefetchScalarGridSpec(
            num_scalar_prefetch=1, grid=(1,), in_specs=[ANY, whole((rows, d)), ANY, whole((rows, d))], out_specs=[ANY] * 2,
            scratch_shapes=[V((rows, d), F32), V((rows, d), F32), pltpu.SemaphoreType.DMA((2,))],
        ),
        out_shape=[jax.ShapeDtypeStruct(y_out.shape, F32)] * 2,
        input_output_aliases={1: 0, 3: 1},
    )(here, y_out, y_got, gr_out, gr_got)

    both = arrived[1] + arrived[0]
    home_mine, home_other, away_mine, away_other = simple(
        last_pair_kernel, here, both, [ANY, HERE, HERE, HERE] * 2,
        [jax.ShapeDtypeStruct((dshare, width), t) for t in (F32, BF, BF, BF)], [whole((dshare, width))] * 4,
        [V((2, share, width), BF), V((2, share, width), F32), pltpu.SemaphoreType.DMA((2,))], SMALL_LIMIT,
    )
    sections = lax.axis_size("section")
    cross = [(s * ranks + i, (s ^ 1) * ranks + (i ^ 1)) for s in range(sections) for i in range(ranks)]
    arrays = [home_mine, paired(away_mine), along(home_other, 1, 2, 1), lax.ppermute(away_other, ("section", "dp"), cross),
              shuffle]
    shapes = [(dshare, joined), (dshare, d), (dshare * fshare, d), (1, dshare), (1, hshare), (1, hshare), (1, dshare * fshare),
              (1, dshare)]
    g_in, g_attn, g_down, g_ng, g_q, g_k, g_ub, g_ob = simple(
        partial(finish_kernel, d, ff), here, arrays, [whole(a.shape) for a in arrays],
        [jax.ShapeDtypeStruct(s, F32) for s in shapes], [whole(s) for s in shapes], [],
    )
    return (y_out.reshape(1, slots * rows, d), gr_out.reshape(1, slots * rows, d), g_in[None], g_attn[None], g_down[None],
            g_ng, g_q, g_k, g_ub, g_ob)


def solution(mesh):
    in_specs = (P("dp", None),) * 3 + (P("section", "dp", None),) * 3 + (P("section", "dp"),) * 5
    out_specs = (P("section", "dp", None),) * 5 + (P("section", "dp"),) * 5
    return jax.shard_map(body, mesh=mesh, in_specs=in_specs, out_specs=out_specs, check_vma=False)
```

profile of v0, /device:TPU:1, one launch (start us, length us, event | category | flops | bytes accessed | tf_op | source)
XLA Modules:
  0.0 467.4 jit_solution(8201807736011997025)
XLA Ops:
  12.4 9.7 %collective-permute-done = bf16[24,9344]{1,0:T(8,128)(2,1)S(1)} collective-permute-done((bf16[24,9344]{1,0:T(8,128)(2,1)}, bf16[24,9344]{1,0:T(8,128)(2,1)S(1)}, u32[]{:S(2)}, u32[]{:S(2)}) %collective-permute-start) | collective-permute-done | bytes 448544 | tf_op jit(solution)/shard_map/ppermute | solution.py:707
  46.2 8.4 %collective-permute-done.5 = bf16[384,256]{1,0:T(8,128)(2,1)S(1)} collective-permute-done((bf16[384,256]{1,0:T(8,128)(2,1)S(1)}, bf16[384,256]{1,0:T(8,128)(2,1)S(1)}, u32[]{:S(2)}, u32[]{:S(2)}) %collective-permute-start.5) | collective-permute-done | bytes 196640 | tf_op jit(solution)/shard_map/ppermute | solution.py:748
  58.7 76.6 %all-gather.3.cloned.1.call-done.refs_1_ = bf16[768,18688]{1,0:T(8,128)(2,1)} async-done(((bf16[24,18688]{1,0:T(8,128)(2,1)}), bf16[768,18688]{1,0:T(8,128)(2,1)}) %all-gather.3.cloned.1.call-update) | async-done | bytes 28704784 | tf_op jit(solution)/shard_map/all_gather | solution.py:744
  135.9 16.7 %shard_map.201 = (bf16[384,768]{1,0:T(8,128)(2,1)}, bf16[384,768]{1,0:T(8,128)(2,1)}, bf16[384,768]{1,0:T(8,128)(2,1)}, bf16[384,768]{1,0:T(8,128)(2,1)}, bf16[3...) custom-call(s32[4]{0:T(128)} %pad_add_fusion.1.idx, ...), custom_call_target="tpu_custom_call", output_to_operand_aliasing={{1}: (6, {}), {2}: (7, {}), {3}: (8, {}), {4}: (9, {}), {5}... | custom-call | flops 1024 | bytes 1024 | tf_op jit(solution)/shard_map/pallas_call | solution.py:659
  152.6 16.6 %shard_map.213 = (bf16[384,768]{1,0:T(8,128)(2,1)}, bf16[384,768]{1,0:T(8,128)(2,1)}, bf16[384,768]{1,0:T(8,128)(2,1)}, bf16[384,768]{1,0:T(8,128)(2,1)}, bf16[3...) custom-call(s32[4]{0:T(128)} %get-tuple-element.141.idx, ...), custom_call_target="tpu_custom_call", output_to_operand_aliasing={{1}: (6, {}), {2}: (7, {}), {3}: (8, {}), {4}: (9, {}), {5}... | custom-call | flops 1024 | bytes 1024 | tf_op jit(solution)/shard_map/pallas_call | solution.py:659
  170.6 13.1 %collective-permute-done.6.refs_0_ = bf16[384,768]{1,0:T(8,128)(2,1)S(1)} collective-permute-done((bf16[384,768]{1,0:T(8,128)(2,1)}, bf16[384,768]{1,0:T(8,128)(2,1)S(1)}, u32[]{:S(2)}, u32[]{:S(2)}) %collective-permute-start.6) | collective-permute-done | bytes 589856 | tf_op jit(solution)/shard_map/ppermute | solution.py:805
  187.5 7.6 %shard_map.215 = (bf16[384,768]{1,0:T(8,128)(2,1)}, bf16[384,768]{1,0:T(8,128)(2,1)}, bf16[384,768]{1,0:T(8,128)(2,1)}, bf16[384,768]{1,0:T(8,128)(2,1)}, bf16[3...) custom-call(s32[4]{0:T(128)} %get-tuple-element.139.idx, ...), custom_call_target="tpu_custom_call", output_to_operand_aliasing={{1}: (6, {}), {2}: (7, {}), {3}: (8, {}), {4}: (9, {}), {5}... | custom-call | flops 1024 | bytes 1024 | tf_op jit(solution)/shard_map/pallas_call | solution.py:659
  195.1 18.2 %shard_map.218 = (bf16[384,768]{1,0:T(8,128)(2,1)}, bf16[400,6144]{1,0:T(8,128)(2,1)}, bf16[400,6144]{1,0:T(8,128)(2,1)}, f32[2,384,768]{2,1,0:T(8,128)}, bf16[384,768]{1,0:T(8,128)(2,1)}) custom-call(s32[4]{0:T(128)} %get-tuple-element.139.idx, ...), custom_call_target="tpu_custom_call", output_to_operand_aliasing={{1}: (15, {}), {2}: (16, {}), {3}: (17, {}), {4}: (18, {})} | custom-call | flops 1024 | bytes 1024 | tf_op jit(solution)/shard_map/pallas_call | solution.py:659
  213.3 9.6 %shard_map.219 = (bf16[384,768]{1,0:T(8,128)(2,1)}, bf16[400,6144]{1,0:T(8,128)(2,1)}, bf16[400,6144]{1,0:T(8,128)(2,1)}, f32[2,384,768]{2,1,0:T(8,128)}, bf16[384,768]{1,0:T(8,128)(2,1)}) custom-call(s32[4]{0:T(128)} %pad_add_fusion.idx, ...), custom_call_target="tpu_custom_call", output_to_operand_aliasing={{1}: (15, {}), {2}: (16, {}), {3}: (17, {}), {4}: (18, {})} | custom-call | flops 1024 | bytes 1024 | tf_op jit(solution)/shard_map/pallas_call | solution.py:659
  225.5 53.6 %collective-permute-done.7.refs_0_ = bf16[384,768]{1,0:T(8,128)(2,1)S(1)} collective-permute-done((bf16[384,768]{1,0:T(8,128)(2,1)}, bf16[384,768]{1,0:T(8,128)(2,1)S(1)}, u32[]{:S(2)}, u32[]{:S(2)}) %collective-permute-start.7) | collective-permute-done | bytes 589856 | tf_op jit(solution)/shard_map/ppermute | solution.py:879
  280.1 21.5 %shard_map.220 = (bf16[384,768]{1,0:T(8,128)(2,1)}, bf16[400,6144]{1,0:T(8,128)(2,1)}, bf16[400,6144]{1,0:T(8,128)(2,1)}, f32[2,384,768]{2,1,0:T(8,128)}, bf16[384,768]{1,0:T(8,128)(2,1)}) custom-call(s32[4]{0:T(128)} %get-tuple-element.141.idx, ...), custom_call_target="tpu_custom_call", output_to_operand_aliasing={{1}: (15, {}), {2}: (16, {}), {3}: (17, {}), {4}: (18, {})} | custom-call | flops 1024 | bytes 1024 | tf_op jit(solution)/shard_map/pallas_call | solution.py:659
  302.9 21.0 %shard_map.221 = (bf16[384,768]{1,0:T(8,128)(2,1)}, bf16[400,6144]{1,0:T(8,128)(2,1)}, bf16[400,6144]{1,0:T(8,128)(2,1)}, f32[2,384,768]{2,1,0:T(8,128)}, bf16[384,768]{1,0:T(8,128)(2,1)}) custom-call(s32[4]{0:T(128)} %pad_add_fusion.1.idx, ...), custom_call_target="tpu_custom_call", output_to_operand_aliasing={{1}: (15, {}), {2}: (16, {}), {3}: (17, {}), {4}: (18, {})} | custom-call | flops 1024 | bytes 1024 | tf_op jit(solution)/shard_map/pallas_call | solution.py:659
  326.2 11.9 %shard_map.222 = (bf16[192,4736]{1,0:T(8,128)(2,1)}, bf16[192,4736]{1,0:T(8,128)(2,1)}, bf16[192,4736]{1,0:T(8,128)(2,1)}, bf16[96,4736]{1,0:T(8,128)(2,1)}, bf16[96,4736]{1,0:T(8,128)(2,1)}) custom-call(s32[5]{0:T(128)} %stack.83.idx, bf16[400,6144]{1,0:T(8,128)(2,1)} %get-tuple-element.217.kept, bf16[400,6144]{1,0:T(8,128)(2,1)} %copy-done.10), custom_call_target="tpu_custom_call" | custom-call | flops 1024 | bytes 1024 | tf_op jit(solution)/shard_map/pallas_call | solution.py:685
  341.7 12.4 %shard_map.224 = (bf16[192,4736]{1,0:T(8,128)(2,1)}, bf16[192,4736]{1,0:T(8,128)(2,1)}, bf16[192,4736]{1,0:T(8,128)(2,1)}, bf16[96,4736]{1,0:T(8,128)(2,1)}, bf16[96,4736]{1,0:T(8,128)(2,1)}) custom-call(s32[5]{0:T(128)} %stack.83.idx, bf16[400,6144]{1,0:T(8,128)(2,1)} %get-tuple-element.230.kept, bf16[400,6144]{1,0:T(8,128)(2,1)} %collective-permute-done.11.got), custom_call_target="tpu_custom_call" | custom-call | flops 1024 | bytes 1024 | tf_op jit(solution)/shard_map/pallas_call | solution.py:685
  363.5 4.8 %collective-permute-done.12.up_got = bf16[96,4736]{1,0:T(8,128)(2,1)S(1)} collective-permute-done((bf16[96,4736]{1,0:T(8,128)(2,1)}, bf16[96,4736]{1,0:T(8,128)(2,1)S(1)}, u32[]{:S(2)}, u32[]{:S(2)}) %collective-permute-start.12) | collective-permute-done | bytes 909344 | tf_op jit(solution)/shard_map/ppermute | solution.py:819
  373.6 14.2 %collective-permute-done.21.refs_1_ = bf16[192,4736]{1,0:T(8,128)(2,1)S(1)} collective-permute-done((bf16[192,4736]{1,0:T(8,128)(2,1)S(1)}, bf16[192,4736]{1,0:T(8,128)(2,1)S(1)}, u32[]{:S(2)}, u32[]{:S(2)}) %collective-permute-start.21) | collective-permute-done | bytes 1818656 | tf_op jit(solution)/shard_map/ppermute | solution.py:819
  389.0 4.5 shard_map.228
  398.0 19.1 %collective-permute-done.14.refs_1_ = bf16[192,4736]{1,0:T(8,128)(2,1)} collective-permute-done((bf16[192,4736]{1,0:T(8,128)(2,1)S(1)}, bf16[192,4736]{1,0:T(8,128)(2,1)}, u32[]{:S(2)}, u32[]{:S(2)}) %collective-permute-start.14) | collective-permute-done | bytes 1818656 | tf_op jit(solution)/shard_map/ppermute | solution.py:819
  417.1 4.6 shard_map.226
  426.2 4.6 collective-permute-done.16.refs_1_
  430.8 5.8 %collective-permute-done.17.refs_2_ = bf16[48,4736]{1,0:T(8,128)(2,1)S(1)} collective-permute-done((bf16[48,4736]{1,0:T(8,128)(2,1)}, bf16[48,4736]{1,0:T(8,128)(2,1)S(1)}, u32[]{:S(2)}, u32[]{:S(2)}) %collective-permute-start.17) | collective-permute-done | bytes 454688 | tf_op jit(solution)/shard_map/ppermute | solution.py:819
  440.7 4.6 collective-permute-start.27
  450.1 4.9 %collective-permute-done.28.c_in = bf16[24,4736]{1,0:T(8,128)(2,1)S(1)} collective-permute-done((bf16[24,4736]{1,0:T(8,128)(2,1)S(1)}, bf16[24,4736]{1,0:T(8,128)(2,1)S(1)}, u32[]{:S(2)}, u32[]{:S(2)}) %collective-permute-start.28) | collective-permute-done | bytes 227360 | tf_op jit(solution)/shard_map/ppermute | solution.py:912
  455.7 4.7 shard_map.230
  (146 shorter events, 84.0 us)
Async XLA Ops:
  7.2 128.1 %all-gather.3.cloned.1.call-start = ((), (), s32[]{:S(2)}) async-start(), calls=%async_computation | async-start | bytes 29601792 | tf_op jit(solution)/shard_map/all_gather | solution.py:744
  10.4 11.8 %collective-permute-start = (bf16[24,9344]{1,0:T(8,128)(2,1)}, bf16[24,9344]{1,0:T(8,128)(2,1)S(1)}, u32[]{:S(2)}, u32[]{:S(2)}) collective-permute-start(bf16[24,9344]{1,0:T(8,128)(2,1)} %shard_map.186), channel_id=1, source_target_pairs={{0,32},{32,0},{64,96},{96,64},{1,33},{33,1},{65,97},{97,65},{2,34}... | collective-permute-start | bytes 1345544 | tf_op jit(solution)/shard_map/ppermute | solution.py:707
  42.5 12.1 %collective-permute-start.5 = (bf16[384,256]{1,0:T(8,128)(2,1)S(1)}, bf16[384,256]{1,0:T(8,128)(2,1)S(1)}, u32[]{:S(2)}, u32[]{:S(2)}) collective-permute-start(bf16[384,256]{1,0:T(8,128)(2,1)S(1)} %maximum_select_fusion.1), channel_id=1, source_target_pairs={{0,16},{1,17},{2,18},{3,19},{4,20},{5,21},{6,22},{7,23},{8,24},{9,... | collective-permute-start | bytes 589832 | tf_op jit(solution)/shard_map/ppermute | solution.py:748
  169.3 14.4 %collective-permute-start.6 = (bf16[384,768]{1,0:T(8,128)(2,1)}, bf16[384,768]{1,0:T(8,128)(2,1)S(1)}, u32[]{:S(2)}, u32[]{:S(2)}) collective-permute-start(bf16[384,768]{1,0:T(8,128)(2,1)} %get-tuple-element.149), channel_id=1, source_target_pairs={{0,96},{32,64},{1,97},{33,65},{2,98},{34,66},{3,99},{35,67},{4,100... | collective-permute-start | bytes 1769480 | tf_op jit(solution)/shard_map/ppermute | solution.py:805
  223.0 56.1 %collective-permute-start.7 = (bf16[384,768]{1,0:T(8,128)(2,1)}, bf16[384,768]{1,0:T(8,128)(2,1)S(1)}, u32[]{:S(2)}, u32[]{:S(2)}) collective-permute-start(bf16[384,768]{1,0:T(8,128)(2,1)} %get-tuple-element.203), channel_id=1, source_target_pairs={{96,0},{64,32},{97,1},{65,33},{98,2},{66,34},{99,3},{67,35},{100,4... | collective-permute-start | bytes 1769480 | tf_op jit(solution)/shard_map/ppermute | solution.py:879
  224.3 54.8 %collective-permute-start.8 = (bf16[384,768]{1,0:T(8,128)(2,1)S(1)}, bf16[384,768]{1,0:T(8,128)(2,1)S(1)}, u32[]{:S(2)}, u32[]{:S(2)}) collective-permute-start(bf16[384,768]{1,0:T(8,128)(2,1)S(1)} %copy-done.9), channel_id=1, source_target_pairs={{0,32},{32,0},{64,96},{96,64},{1,33},{33,1},{65,97},{97,65},{2,34}... | collective-permute-start | bytes 1769480 | tf_op jit(solution)/shard_map/ppermute | solution.py:707
  301.6 22.4 %collective-permute-start.9 = (bf16[400,6144]{1,0:T(8,128)(2,1)}, bf16[400,6144]{1,0:T(8,128)(2,1)S(1)}, u32[]{:S(2)}, u32[]{:S(2)}) collective-permute-start(bf16[400,6144]{1,0:T(8,128)(2,1)} %get-tuple-element.219), channel_id=1, source_target_pairs={{0,1},{1,0},{2,3},{3,2},{4,5},{5,4},{6,7},{7,6},{8,9},{9,8},{10,11... | collective-permute-start | bytes 14745608 | tf_op jit(solution)/shard_map/ppermute | solution.py:703
  324.0 17.7 %collective-permute-start.11 = (bf16[400,6144]{1,0:T(8,128)(2,1)}, bf16[400,6144]{1,0:T(8,128)(2,1)}, u32[]{:S(2)}, u32[]{:S(2)}) collective-permute-start(bf16[400,6144]{1,0:T(8,128)(2,1)} %get-tuple-element.231), channel_id=1, source_target_pairs={{0,1},{1,0},{2,3},{3,2},{4,5},{5,4},{6,7},{7,6},{8,9},{9,8},{10,11... | collective-permute-start | bytes 14745608 | tf_op jit(solution)/shard_map/ppermute | solution.py:703
  324.1 14.8 %collective-permute-start.10 = (bf16[384,768]{1,0:T(8,128)(2,1)}, bf16[384,768]{1,0:T(8,128)(2,1)S(1)}, u32[]{:S(2)}, u32[]{:S(2)}) collective-permute-start(bf16[384,768]{1,0:T(8,128)(2,1)} %get-tuple-element.226), channel_id=1, source_target_pairs={{0,32},{32,0},{64,96},{96,64},{1,33},{33,1},{65,97},{97,65},{2,34}... | collective-permute-start | bytes 1769480 | tf_op jit(solution)/shard_map/ppermute | solution.py:707
  338.9 18.2 %collective-permute-start.19 = (bf16[96,4736]{1,0:T(8,128)(2,1)}, bf16[96,4736]{1,0:T(8,128)(2,1)S(1)}, u32[]{:S(2)}, u32[]{:S(2)}) collective-permute-start(bf16[96,4736]{1,0:T(8,128)(2,1)} %get-tuple-element.246), channel_id=1, source_target_pairs={{0,8},{1,3},{2,10},{3,5},{4,12},{5,7},{6,14},{7,1},{8,16},{9,11},{... | collective-permute-start | bytes 2727944 | tf_op jit(solution)/shard_map/ppermute | solution.py:819
  339.5 17.6 %collective-permute-start.20 = (bf16[96,4736]{1,0:T(8,128)(2,1)}, bf16[96,4736]{1,0:T(8,128)(2,1)}, u32[]{:S(2)}, u32[]{:S(2)}) collective-permute-start(bf16[96,4736]{1,0:T(8,128)(2,1)} %get-tuple-element.247), channel_id=1, source_target_pairs={{0,24},{1,7},{2,26},{3,1},{4,28},{5,3},{6,30},{7,5},{8,0},{9,15},{... | collective-permute-start | bytes 2727944 | tf_op jit(solution)/shard_map/ppermute | solution.py:819
  354.1 14.2 %collective-permute-start.12 = (bf16[96,4736]{1,0:T(8,128)(2,1)}, bf16[96,4736]{1,0:T(8,128)(2,1)S(1)}, u32[]{:S(2)}, u32[]{:S(2)}) collective-permute-start(bf16[96,4736]{1,0:T(8,128)(2,1)} %get-tuple-element.235), channel_id=1, source_target_pairs={{0,8},{1,3},{2,10},{3,5},{4,12},{5,7},{6,14},{7,1},{8,16},{9,11},{... | collective-permute-start | bytes 2727944 | tf_op jit(solution)/shard_map/ppermute | solution.py:819
  354.4 13.8 %collective-permute-start.13 = (bf16[96,4736]{1,0:T(8,128)(2,1)}, bf16[96,4736]{1,0:T(8,128)(2,1)S(1)}, u32[]{:S(2)}, u32[]{:S(2)}) collective-permute-start(bf16[96,4736]{1,0:T(8,128)(2,1)} %get-tuple-element.236), channel_id=1, source_target_pairs={{0,24},{1,7},{2,26},{3,1},{4,28},{5,3},{6,30},{7,5},{8,0},{9,15},{... | collective-permute-start | bytes 2727944 | tf_op jit(solution)/shard_map/ppermute | solution.py:819
  360.8 27.0 %collective-permute-start.21 = (bf16[192,4736]{1,0:T(8,128)(2,1)S(1)}, bf16[192,4736]{1,0:T(8,128)(2,1)S(1)}, u32[]{:S(2)}, u32[]{:S(2)}) collective-permute-start(bf16[192,4736]{1,0:T(8,128)(2,1)S(1)} %get-tuple-element.248), channel_id=1, source_target_pairs={{0,8},{1,3},{2,10},{3,5},{4,12},{5,7},{6,14},{7,1},{8,16},{9,11},{... | collective-permute-start | bytes 5455880 | tf_op jit(solution)/shard_map/ppermute | solution.py:819
  360.9 28.2 %collective-permute-start.22 = (bf16[192,4736]{1,0:T(8,128)(2,1)S(1)}, bf16[192,4736]{1,0:T(8,128)(2,1)}, u32[]{:S(2)}, u32[]{:S(2)}) collective-permute-start(bf16[192,4736]{1,0:T(8,128)(2,1)S(1)} %get-tuple-element.249), channel_id=1, source_target_pairs={{0,24},{1,7},{2,26},{3,1},{4,28},{5,3},{6,30},{7,5},{8,0},{9,15},{... | collective-permute-start | bytes 5455880 | tf_op jit(solution)/shard_map/ppermute | solution.py:819
  370.8 46.3 %collective-permute-start.14 = (bf16[192,4736]{1,0:T(8,128)(2,1)S(1)}, bf16[192,4736]{1,0:T(8,128)(2,1)}, u32[]{:S(2)}, u32[]{:S(2)}) collective-permute-start(bf16[192,4736]{1,0:T(8,128)(2,1)S(1)} %get-tuple-element.237), channel_id=1, source_target_pairs={{0,8},{1,3},{2,10},{3,5},{4,12},{5,7},{6,14},{7,1},{8,16},{9,11},{... | collective-permute-start | bytes 5455880 | tf_op jit(solution)/shard_map/ppermute | solution.py:819
  370.9 46.2 %collective-permute-start.15 = (bf16[192,4736]{1,0:T(8,128)(2,1)S(1)}, bf16[192,4736]{1,0:T(8,128)(2,1)}, u32[]{:S(2)}, u32[]{:S(2)}) collective-permute-start(bf16[192,4736]{1,0:T(8,128)(2,1)S(1)} %get-tuple-element.238), channel_id=1, source_target_pairs={{0,24},{1,7},{2,26},{3,1},{4,28},{5,3},{6,30},{7,5},{8,0},{9,15},{... | collective-permute-start | bytes 5455880 | tf_op jit(solution)/shard_map/ppermute | solution.py:819
  393.5 31.8 %collective-permute-start.23 = (bf16[48,4736]{1,0:T(8,128)(2,1)}, bf16[48,4736]{1,0:T(8,128)(2,1)S(1)}, u32[]{:S(2)}, u32[]{:S(2)}) collective-permute-start(bf16[48,4736]{1,0:T(8,128)(2,1)} %get-tuple-element.251), channel_id=1, source_target_pairs={{0,2},{1,9},{2,4},{3,11},{4,6},{5,13},{6,0},{7,15},{8,10},{9,17},{... | collective-permute-start | bytes 1363976 | tf_op jit(solution)/shard_map/ppermute | solution.py:819
  394.4 31.8 %collective-permute-start.24 = (bf16[48,4736]{1,0:T(8,128)(2,1)}, bf16[48,4736]{1,0:T(8,128)(2,1)S(1)}, u32[]{:S(2)}, u32[]{:S(2)}) collective-permute-start(bf16[48,4736]{1,0:T(8,128)(2,1)} %get-tuple-element.252), channel_id=1, source_target_pairs={{0,4},{1,17},{2,6},{3,19},{4,0},{5,21},{6,2},{7,23},{8,12},{9,25},... | collective-permute-start | bytes 1363976 | tf_op jit(solution)/shard_map/ppermute | solution.py:819
  397.3 29.0 %collective-permute-start.25 = (bf16[48,4736]{1,0:T(8,128)(2,1)}, bf16[48,4736]{1,0:T(8,128)(2,1)S(1)}, u32[]{:S(2)}, u32[]{:S(2)}) collective-permute-start(bf16[48,4736]{1,0:T(8,128)(2,1)} %get-tuple-element.253), channel_id=1, source_target_pairs={{0,6},{1,25},{2,0},{3,27},{4,2},{5,29},{6,4},{7,31},{8,14},{9,1},{... | collective-permute-start | bytes 1363976 | tf_op jit(solution)/shard_map/ppermute | solution.py:819
  422.6 13.9 %collective-permute-start.17 = (bf16[48,4736]{1,0:T(8,128)(2,1)}, bf16[48,4736]{1,0:T(8,128)(2,1)S(1)}, u32[]{:S(2)}, u32[]{:S(2)}) collective-permute-start(bf16[48,4736]{1,0:T(8,128)(2,1)} %get-tuple-element.241), channel_id=1, source_target_pairs={{0,4},{1,17},{2,6},{3,19},{4,0},{5,21},{6,2},{7,23},{8,12},{9,25},... | collective-permute-start | bytes 1363976 | tf_op jit(solution)/shard_map/ppermute | solution.py:819
  425.3 11.2 %collective-permute-start.18 = (bf16[48,4736]{1,0:T(8,128)(2,1)}, bf16[48,4736]{1,0:T(8,128)(2,1)S(1)}, u32[]{:S(2)}, u32[]{:S(2)}) collective-permute-start(bf16[48,4736]{1,0:T(8,128)(2,1)} %get-tuple-element.242), channel_id=1, source_target_pairs={{0,6},{1,25},{2,0},{3,27},{4,2},{5,29},{6,4},{7,31},{8,14},{9,1},{... | collective-permute-start | bytes 1363976 | tf_op jit(solution)/shard_map/ppermute | solution.py:819
  440.6 9.5 %collective-permute-start.26 = (bf16[24,4736]{1,0:T(8,128)(2,1)S(1)}, bf16[24,4736]{1,0:T(8,128)(2,1)S(1)}, u32[]{:S(2)}, u32[]{:S(2)}) collective-permute-start(bf16[24,4736]{1,0:T(8,128)(2,1)S(1)} %get-tuple-element.255), channel_id=1, source_target_pairs={{0,32},{32,0},{64,96},{96,64},{1,33},{33,1},{65,97},{97,65},{2,34}... | collective-permute-start | bytes 681992 | tf_op jit(solution)/shard_map/ppermute | solution.py:707
  445.3 9.7 %collective-permute-start.28 = (bf16[24,4736]{1,0:T(8,128)(2,1)S(1)}, bf16[24,4736]{1,0:T(8,128)(2,1)S(1)}, u32[]{:S(2)}, u32[]{:S(2)}) collective-permute-start(bf16[24,4736]{1,0:T(8,128)(2,1)S(1)} %get-tuple-element.257), channel_id=1, source_target_pairs={{0,33},{1,32},{2,35},{3,34},{4,37},{5,36},{6,39},{7,38},{8,41},{9,... | collective-permute-start | bytes 681992 | tf_op jit(solution)/shard_map/ppermute | solution.py:912
  (26 other events, 196.7 us)
Sparse Core Ops, SparseCore 0:
  24.3 110.9 all-gather.2
where the time goes:
time: 471 us; the launch traced here: 467 us
  waiting for transfers between devices  221 us (47%)
  Pallas kernels  169 us (36%)
  starting transfers between devices  45.4 us (10%)
  between operations  14.8 us (3%)
  local copies, waits for them, and re-layouts  9.87 us (2%)
  other arithmetic  7.35 us (2%)
    pallas_call x8, Pallas kernels, call(): pl.pallas_call(kernel, grid_spec=pltpu.PrefetchScalarGridSpec(num_scalar_...  114 us
    all_gather x1, waiting for transfers between devices, body(): lax.all_gather(jnp.concatenate([local, other], axis=1), 'dp', axis=0)  76.6 us
    ppermute x1, waiting for transfers between devices, body(): here_g = lax.ppermute(gbf, 'section', [(3, 0), (2, 1)]) if t == 1 else gbf  53.6 us
    ppermute x14, waiting for transfers between devices, moved(): return lax.ppermute(x, 'dp', [(i, to(i)) for i in range(ranks)])  48.3 us
    pallas_call x6, Pallas kernels, simple(): pl.pallas_call(kernel, grid_spec=pltpu.PrefetchScalarGridSpec(num_scalar_...  40.2 us
    ppermute x14, starting transfers between devices, moved(): return lax.ppermute(x, 'dp', [(i, to(i)) for i in range(ranks)])  20.3 us
    ppermute x5, waiting for transfers between devices, body(): got = lax.ppermute(shares, 'dp', [(i, i ^ step) for i in range(ranks)])  13.9 us
    ppermute x1, waiting for transfers between devices, body(): here_x = lax.ppermute(ybf, 'section', [(0, 3), (1, 2)]) if t == 1 else ybf  13.1 us
  transfers between devices with their start and end apart: 30, of which 16 were waited for; matrix products, arithmetic and copies ran while one was open for 1% of the time, Pallas kernels for 14%

commit v1 on v0

--- a/solution.py
+++ b/solution.py
@@ -145,7 +145,7 @@
     spread = head_spread(64)
     for copy in small_copies:
         copy.wait()
-    ids_row = id_v[0:1]
+    ids_row = id_v[...]
     ids_col = as_column(ids_row)
     keep = jnp.where(ids_col < ABSENT, 1.0, 0.0)
     if kind == ARRIVED:
@@ -271,7 +271,7 @@
     spread = head_spread(64)
     for copy in small_copies:
         copy.wait()
-    keep = jnp.where(as_column(id_v[0:1]) < ABSENT, 1.0, 0.0)
+    keep = jnp.where(as_column(id_v[...]) < ABSENT, 1.0, 0.0)
     if kind == ARRIVED:
         g_v[...] = g_in[...]
     else:
@@ -742,20 +742,22 @@
     local = plain(partial(prepare_kernel, d, ff), shares, [full(a) for a in shares], local, full(local), [])
     other = paired(local)
     g = lax.all_gather(jnp.concatenate([local, other], axis=1), "dp", axis=0).reshape(d, 2 * stride)
-    shares = jnp.concatenate([local[:, wide:], other[:, wide:]], axis=1)
+    shares = jnp.concatenate([a[:, wide : wide + 8].reshape(1, 8 * dshare) for a in (local, other)], axis=1)
     step = 1
     while step < ranks:
         got = lax.ppermute(shares, "dp", [(i, i ^ step) for i in range(ranks)])
         low = lax.rem(rank // step, 2) == 0
         shares = jnp.where(low, jnp.concatenate([shares, got]), jnp.concatenate([got, shares]))
         step *= 2
+    shares = shares.reshape(ranks, 2, dshare, 8).transpose(0, 2, 1, 3).reshape(d, 2, 8)
+    shares = jnp.pad(shares, ((0, 0), (0, 0), (0, LANES - 8))).reshape(d, 2 * LANES)
     toks = tokens.reshape(slots, rows, d)
     seeds = cotangent.reshape(slots, rows, d)
     ends = jnp.cumsum(lengths, axis=-1)
     position = jnp.arange(rows, dtype=jnp.int32)
     image = jnp.sum((position[None, :, None] >= ends[:, None, :]).astype(jnp.int32), axis=-1)
     image = jnp.where(position[None, :] < ends[:, 2:3], image, ABSENT + position[None, :])
-    ids = jnp.broadcast_to(image[:, None, :].astype(F32), (slots, 8, rows))
+    ids = image[:, None, :].astype(F32)
 
     def index_of(layer, active_stage):
         return jnp.stack([stage == active_stage, core, slot, odd == layer]).astype(jnp.int32)
@@ -797,7 +799,7 @@
             kept[layer][:9] + operands[layer] + results,
             [V((rows, d), BF), V((rows, d), BF)] + weights_v
             + [V((rows, d), BF)] * 3 + [V((rows, 2 * d), BF)] * 2 + [V((chunks, rows, fc), BF)] * 2
-            + [V((heads, rows, rows), BF), V((16, rows), F32), V((rows, d), BF), V((rows, d), F32), V((rows, d), F32), V((rows, d), BF), V((8, rows), F32), V((8, ff), F32)]
+            + [V((heads, rows, rows), BF), V((16, rows), F32), V((rows, d), BF), V((rows, d), F32), V((rows, d), F32), V((rows, d), BF), V((1, rows), F32), V((8, ff), F32)]
             + sems,
             1 << 10,
         )
@@ -871,7 +873,7 @@
             + [V((rows, d), BF)] * 4 + [V((rows, 2 * d), BF)] * 2
             + [V((chunks, rows, fc), BF), V((heads, rows, rows), BF), V((16, rows), F32)]
             + [V((d, rows), BF), V((d, rows), F32), V((rows, d), F32)]
-            + [V((rows, d), BF)] * 3 + [V((chunks, rows, fc), BF), V((rows, d), F32), V((rows, d), F32), V((rows, d), BF), V((1, stacked), F32), V((16, stacked), BF), V((8, rows), F32), V((8, ff), F32)]
+            + [V((rows, d), BF)] * 3 + [V((chunks, rows, fc), BF), V((rows, d), F32), V((rows, d), F32), V((rows, d), BF), V((1, stacked), F32), V((16, stacked), BF), V((1, rows), F32), V((8, ff), F32)]
             + sems,
             1 << 10,
         )

time: 471 us -> 466 us (0.989)
  waiting for transfers between devices: 221 us -> 213 us
    ppermute x5, waiting for transfers between devices: 13.9 us -> 4.57 us  [body(): got = lax.ppermute(shares, 'dp', [(i, i ^ step) for i in range(ranks)])]
  transfers between devices with their start and end apart: 30 -> 30, of which waited for: 16 -> 16; matrix products, arithmetic and copies ran while one was open for 1% -> 2% of each run, Pallas kernels for 14% -> 14%
where the time goes in v1:
time: 466 us; the launch traced here: 461 us
  waiting for transfers between devices  213 us (46%)
  Pallas kernels  169 us (36%)
  starting transfers between devices  45.4 us (10%)
  between operations  14.9 us (3%)
  local copies, waits for them, and re-layouts  11.8 us (3%)
  other arithmetic  7.38 us (2%)
    pallas_call x8, Pallas kernels, call(): pl.pallas_call(kernel, grid_spec=pltpu.PrefetchScalarGridSpec(num_scalar_...  114 us
    all_gather x1, waiting for transfers between devices, body(): lax.all_gather(jnp.concatenate([local, other], axis=1), 'dp', axis=0)  77.9 us
    ppermute x1, waiting for transfers between devices, body(): here_g = lax.ppermute(gbf, 'section', [(3, 0), (2, 1)]) if t == 1 else gbf  53.3 us
    ppermute x14, waiting for transfers between devices, moved(): return lax.ppermute(x, 'dp', [(i, to(i)) for i in range(ranks)])  48.3 us
    pallas_call x6, Pallas kernels, simple(): pl.pallas_call(kernel, grid_spec=pltpu.PrefetchScalarGridSpec(num_scalar_...  40.2 us
    ppermute x14, starting transfers between devices, moved(): return lax.ppermute(x, 'dp', [(i, to(i)) for i in range(ranks)])  20.4 us
    ppermute x1, waiting for transfers between devices, body(): here_x = lax.ppermute(ybf, 'section', [(0, 3), (1, 2)]) if t == 1 else ybf  13 us
    ppermute x5, starting transfers between devices, body(): got = lax.ppermute(shares, 'dp', [(i, i ^ step) for i in range(ranks)])  11.5 us
  transfers between devices with their start and end apart: 30, of which 16 were waited for; matrix products, arithmetic and copies ran while one was open for 2% of the time, Pallas kernels for 14%

profile of v1, /device:TPU:1, one launch (start us, length us, event | category | flops | bytes accessed | tf_op | source)
XLA Modules:
  0.0 461.3 jit_solution(2481292234705730334)
XLA Ops:
  12.4 9.7 %collective-permute-done = bf16[24,9344]{1,0:T(8,128)(2,1)S(1)} collective-permute-done((bf16[24,9344]{1,0:T(8,128)(2,1)}, bf16[24,9344]{1,0:T(8,128)(2,1)S(1)}, u32[]{:S(2)}, u32[]{:S(2)}) %collective-permute-start) | collective-permute-done | bytes 448544 | tf_op jit(solution)/shard_map/ppermute | solution.py:707
  51.9 77.9 %all-gather.3.cloned.1.call-done.refs_1_ = bf16[768,18688]{1,0:T(8,128)(2,1)} async-done(((bf16[24,18688]{1,0:T(8,128)(2,1)}), bf16[768,18688]{1,0:T(8,128)(2,1)}) %all-gather.3.cloned.1.call-update) | async-done | bytes 28704784 | tf_op jit(solution)/shard_map/all_gather | solution.py:744
  129.8 16.7 %shard_map.201 = (bf16[384,768]{1,0:T(8,128)(2,1)}, bf16[384,768]{1,0:T(8,128)(2,1)}, bf16[384,768]{1,0:T(8,128)(2,1)}, bf16[384,768]{1,0:T(8,128)(2,1)}, bf16[3...) custom-call(s32[4]{0:T(128)} %pad_add_fusion.1.idx, ...), custom_call_target="tpu_custom_call", output_to_operand_aliasing={{1}: (6, {}), {2}: (7, {}), {3}: (8, {}), {4}: (9, {}), {5}... | custom-call | flops 1024 | bytes 1024 | tf_op jit(solution)/shard_map/pallas_call | solution.py:659
  146.5 16.6 %shard_map.213 = (bf16[384,768]{1,0:T(8,128)(2,1)}, bf16[384,768]{1,0:T(8,128)(2,1)}, bf16[384,768]{1,0:T(8,128)(2,1)}, bf16[384,768]{1,0:T(8,128)(2,1)}, bf16[3...) custom-call(s32[4]{0:T(128)} %get-tuple-element.141.idx, ...), custom_call_target="tpu_custom_call", output_to_operand_aliasing={{1}: (6, {}), {2}: (7, {}), {3}: (8, {}), {4}: (9, {}), {5}... | custom-call | flops 1024 | bytes 1024 | tf_op jit(solution)/shard_map/pallas_call | solution.py:659
  164.5 13.0 %collective-permute-done.6.refs_0_ = bf16[384,768]{1,0:T(8,128)(2,1)S(1)} collective-permute-done((bf16[384,768]{1,0:T(8,128)(2,1)}, bf16[384,768]{1,0:T(8,128)(2,1)S(1)}, u32[]{:S(2)}, u32[]{:S(2)}) %collective-permute-start.6) | collective-permute-done | bytes 589856 | tf_op jit(solution)/shard_map/ppermute | solution.py:807
  181.4 7.6 %shard_map.215 = (bf16[384,768]{1,0:T(8,128)(2,1)}, bf16[384,768]{1,0:T(8,128)(2,1)}, bf16[384,768]{1,0:T(8,128)(2,1)}, bf16[384,768]{1,0:T(8,128)(2,1)}, bf16[3...) custom-call(s32[4]{0:T(128)} %get-tuple-element.139.idx, ...), custom_call_target="tpu_custom_call", output_to_operand_aliasing={{1}: (6, {}), {2}: (7, {}), {3}: (8, {}), {4}: (9, {}), {5}... | custom-call | flops 1024 | bytes 1024 | tf_op jit(solution)/shard_map/pallas_call | solution.py:659
  189.0 18.3 %shard_map.218 = (bf16[384,768]{1,0:T(8,128)(2,1)}, bf16[400,6144]{1,0:T(8,128)(2,1)}, bf16[400,6144]{1,0:T(8,128)(2,1)}, f32[2,384,768]{2,1,0:T(8,128)}, bf16[384,768]{1,0:T(8,128)(2,1)}) custom-call(s32[4]{0:T(128)} %get-tuple-element.139.idx, ...), custom_call_target="tpu_custom_call", output_to_operand_aliasing={{1}: (15, {}), {2}: (16, {}), {3}: (17, {}), {4}: (18, {})} | custom-call | flops 1024 | bytes 1024 | tf_op jit(solution)/shard_map/pallas_call | solution.py:659
  207.3 9.7 %shard_map.219 = (bf16[384,768]{1,0:T(8,128)(2,1)}, bf16[400,6144]{1,0:T(8,128)(2,1)}, bf16[400,6144]{1,0:T(8,128)(2,1)}, f32[2,384,768]{2,1,0:T(8,128)}, bf16[384,768]{1,0:T(8,128)(2,1)}) custom-call(s32[4]{0:T(128)} %pad_add_fusion.idx, ...), custom_call_target="tpu_custom_call", output_to_operand_aliasing={{1}: (15, {}), {2}: (16, {}), {3}: (17, {}), {4}: (18, {})} | custom-call | flops 1024 | bytes 1024 | tf_op jit(solution)/shard_map/pallas_call | solution.py:659
  219.6 53.3 %collective-permute-done.7.refs_0_ = bf16[384,768]{1,0:T(8,128)(2,1)S(1)} collective-permute-done((bf16[384,768]{1,0:T(8,128)(2,1)}, bf16[384,768]{1,0:T(8,128)(2,1)S(1)}, u32[]{:S(2)}, u32[]{:S(2)}) %collective-permute-start.7) | collective-permute-done | bytes 589856 | tf_op jit(solution)/shard_map/ppermute | solution.py:881
  273.9 21.5 %shard_map.220 = (bf16[384,768]{1,0:T(8,128)(2,1)}, bf16[400,6144]{1,0:T(8,128)(2,1)}, bf16[400,6144]{1,0:T(8,128)(2,1)}, f32[2,384,768]{2,1,0:T(8,128)}, bf16[384,768]{1,0:T(8,128)(2,1)}) custom-call(s32[4]{0:T(128)} %get-tuple-element.141.idx, ...), custom_call_target="tpu_custom_call", output_to_operand_aliasing={{1}: (15, {}), {2}: (16, {}), {3}: (17, {}), {4}: (18, {})} | custom-call | flops 1024 | bytes 1024 | tf_op jit(solution)/shard_map/pallas_call | solution.py:659
  296.8 21.0 %shard_map.221 = (bf16[384,768]{1,0:T(8,128)(2,1)}, bf16[400,6144]{1,0:T(8,128)(2,1)}, bf16[400,6144]{1,0:T(8,128)(2,1)}, f32[2,384,768]{2,1,0:T(8,128)}, bf16[384,768]{1,0:T(8,128)(2,1)}) custom-call(s32[4]{0:T(128)} %pad_add_fusion.1.idx, ...), custom_call_target="tpu_custom_call", output_to_operand_aliasing={{1}: (15, {}), {2}: (16, {}), {3}: (17, {}), {4}: (18, {})} | custom-call | flops 1024 | bytes 1024 | tf_op jit(solution)/shard_map/pallas_call | solution.py:659
  320.1 11.9 %shard_map.222 = (bf16[192,4736]{1,0:T(8,128)(2,1)}, bf16[192,4736]{1,0:T(8,128)(2,1)}, bf16[192,4736]{1,0:T(8,128)(2,1)}, bf16[96,4736]{1,0:T(8,128)(2,1)}, bf16[96,4736]{1,0:T(8,128)(2,1)}) custom-call(s32[5]{0:T(128)} %stack.83.idx, bf16[400,6144]{1,0:T(8,128)(2,1)} %get-tuple-element.217.kept, bf16[400,6144]{1,0:T(8,128)(2,1)} %copy-done.10), custom_call_target="tpu_custom_call" | custom-call | flops 1024 | bytes 1024 | tf_op jit(solution)/shard_map/pallas_call | solution.py:685
  335.6 12.4 %shard_map.224 = (bf16[192,4736]{1,0:T(8,128)(2,1)}, bf16[192,4736]{1,0:T(8,128)(2,1)}, bf16[192,4736]{1,0:T(8,128)(2,1)}, bf16[96,4736]{1,0:T(8,128)(2,1)}, bf16[96,4736]{1,0:T(8,128)(2,1)}) custom-call(s32[5]{0:T(128)} %stack.83.idx, bf16[400,6144]{1,0:T(8,128)(2,1)} %get-tuple-element.230.kept, bf16[400,6144]{1,0:T(8,128)(2,1)} %collective-permute-done.11.got), custom_call_target="tpu_custom_call" | custom-call | flops 1024 | bytes 1024 | tf_op jit(solution)/shard_map/pallas_call | solution.py:685
  351.0 3.6 shard_map.227
  357.4 4.8 %collective-permute-done.12.up_got = bf16[96,4736]{1,0:T(8,128)(2,1)S(1)} collective-permute-done((bf16[96,4736]{1,0:T(8,128)(2,1)}, bf16[96,4736]{1,0:T(8,128)(2,1)S(1)}, u32[]{:S(2)}, u32[]{:S(2)}) %collective-permute-start.12) | collective-permute-done | bytes 909344 | tf_op jit(solution)/shard_map/ppermute | solution.py:821
  367.5 14.2 %collective-permute-done.21.refs_1_ = bf16[192,4736]{1,0:T(8,128)(2,1)S(1)} collective-permute-done((bf16[192,4736]{1,0:T(8,128)(2,1)S(1)}, bf16[192,4736]{1,0:T(8,128)(2,1)S(1)}, u32[]{:S(2)}, u32[]{:S(2)}) %collective-permute-start.21) | collective-permute-done | bytes 1818656 | tf_op jit(solution)/shard_map/ppermute | solution.py:821
  382.9 4.5 shard_map.228
  391.9 19.0 %collective-permute-done.14.refs_1_ = bf16[192,4736]{1,0:T(8,128)(2,1)} collective-permute-done((bf16[192,4736]{1,0:T(8,128)(2,1)S(1)}, bf16[192,4736]{1,0:T(8,128)(2,1)}, u32[]{:S(2)}, u32[]{:S(2)}) %collective-permute-start.14) | collective-permute-done | bytes 1818656 | tf_op jit(solution)/shard_map/ppermute | solution.py:821
  411.0 4.6 shard_map.226
  420.1 4.5 collective-permute-done.16.refs_1_
  424.6 5.8 %collective-permute-done.17.refs_2_ = bf16[48,4736]{1,0:T(8,128)(2,1)S(1)} collective-permute-done((bf16[48,4736]{1,0:T(8,128)(2,1)}, bf16[48,4736]{1,0:T(8,128)(2,1)S(1)}, u32[]{:S(2)}, u32[]{:S(2)}) %collective-permute-start.17) | collective-permute-done | bytes 454688 | tf_op jit(solution)/shard_map/ppermute | solution.py:821
  434.6 4.6 collective-permute-start.27
  444.0 4.9 %collective-permute-done.28.c_in = bf16[24,4736]{1,0:T(8,128)(2,1)S(1)} collective-permute-done((bf16[24,4736]{1,0:T(8,128)(2,1)S(1)}, bf16[24,4736]{1,0:T(8,128)(2,1)S(1)}, u32[]{:S(2)}, u32[]{:S(2)}) %collective-permute-start.28) | collective-permute-done | bytes 227360 | tf_op jit(solution)/shard_map/ppermute | solution.py:914
  449.6 4.7 %shard_map.230 = (f32[24,5376]{1,0:T(8,128)}, f32[24,768]{1,0:T(8,128)}, f32[96,768]{1,0:T(8,128)}, f32[1,24]{1,0:T(1,128)}, f32[1,2]{1,0:T(1,128)}, /*index=5*/...) custom-call(s32[5]{0:T(128)} %stack.83.idx, f32[24,4736]{1,0:T(8,128)} %copy-done.4, bf16[24,4736]{1,0:T(8,128)(2,1)} %copy-done.16, ...), custom_call_target="tpu_custom_call" | custom-call | flops 1024 | bytes 1024 | tf_op jit(solution)/shard_map/pallas_call | solution.py:685
  (164 shorter events, 81.4 us)
Async XLA Ops:
  7.2 122.6 %all-gather.3.cloned.1.call-start = ((), (), s32[]{:S(2)}) async-start(), calls=%async_computation | async-start | bytes 29601792 | tf_op jit(solution)/shard_map/all_gather | solution.py:744
  10.4 11.8 %collective-permute-start = (bf16[24,9344]{1,0:T(8,128)(2,1)}, bf16[24,9344]{1,0:T(8,128)(2,1)S(1)}, u32[]{:S(2)}, u32[]{:S(2)}) collective-permute-start(bf16[24,9344]{1,0:T(8,128)(2,1)} %shard_map.186), channel_id=1, source_target_pairs={{0,32},{32,0},{64,96},{96,64},{1,33},{33,1},{65,97},{97,65},{2,34}... | collective-permute-start | bytes 1345544 | tf_op jit(solution)/shard_map/ppermute | solution.py:707
  163.2 14.4 %collective-permute-start.6 = (bf16[384,768]{1,0:T(8,128)(2,1)}, bf16[384,768]{1,0:T(8,128)(2,1)S(1)}, u32[]{:S(2)}, u32[]{:S(2)}) collective-permute-start(bf16[384,768]{1,0:T(8,128)(2,1)} %get-tuple-element.149), channel_id=1, source_target_pairs={{0,96},{32,64},{1,97},{33,65},{2,98},{34,66},{3,99},{35,67},{4,100... | collective-permute-start | bytes 1769480 | tf_op jit(solution)/shard_map/ppermute | solution.py:807
  217.0 55.9 %collective-permute-start.7 = (bf16[384,768]{1,0:T(8,128)(2,1)}, bf16[384,768]{1,0:T(8,128)(2,1)S(1)}, u32[]{:S(2)}, u32[]{:S(2)}) collective-permute-start(bf16[384,768]{1,0:T(8,128)(2,1)} %get-tuple-element.203), channel_id=1, source_target_pairs={{96,0},{64,32},{97,1},{65,33},{98,2},{66,34},{99,3},{67,35},{100,4... | collective-permute-start | bytes 1769480 | tf_op jit(solution)/shard_map/ppermute | solution.py:881
  218.3 54.6 %collective-permute-start.8 = (bf16[384,768]{1,0:T(8,128)(2,1)S(1)}, bf16[384,768]{1,0:T(8,128)(2,1)S(1)}, u32[]{:S(2)}, u32[]{:S(2)}) collective-permute-start(bf16[384,768]{1,0:T(8,128)(2,1)S(1)} %copy-done.9), channel_id=1, source_target_pairs={{0,32},{32,0},{64,96},{96,64},{1,33},{33,1},{65,97},{97,65},{2,34}... | collective-permute-start | bytes 1769480 | tf_op jit(solution)/shard_map/ppermute | solution.py:707
  295.4 22.4 %collective-permute-start.9 = (bf16[400,6144]{1,0:T(8,128)(2,1)}, bf16[400,6144]{1,0:T(8,128)(2,1)S(1)}, u32[]{:S(2)}, u32[]{:S(2)}) collective-permute-start(bf16[400,6144]{1,0:T(8,128)(2,1)} %get-tuple-element.219), channel_id=1, source_target_pairs={{0,1},{1,0},{2,3},{3,2},{4,5},{5,4},{6,7},{7,6},{8,9},{9,8},{10,11... | collective-permute-start | bytes 14745608 | tf_op jit(solution)/shard_map/ppermute | solution.py:703
  317.9 17.7 %collective-permute-start.11 = (bf16[400,6144]{1,0:T(8,128)(2,1)}, bf16[400,6144]{1,0:T(8,128)(2,1)}, u32[]{:S(2)}, u32[]{:S(2)}) collective-permute-start(bf16[400,6144]{1,0:T(8,128)(2,1)} %get-tuple-element.231), channel_id=1, source_target_pairs={{0,1},{1,0},{2,3},{3,2},{4,5},{5,4},{6,7},{7,6},{8,9},{9,8},{10,11... | collective-permute-start | bytes 14745608 | tf_op jit(solution)/shard_map/ppermute | solution.py:703
  318.0 14.8 %collective-permute-start.10 = (bf16[384,768]{1,0:T(8,128)(2,1)}, bf16[384,768]{1,0:T(8,128)(2,1)S(1)}, u32[]{:S(2)}, u32[]{:S(2)}) collective-permute-start(bf16[384,768]{1,0:T(8,128)(2,1)} %get-tuple-element.226), channel_id=1, source_target_pairs={{0,32},{32,0},{64,96},{96,64},{1,33},{33,1},{65,97},{97,65},{2,34}... | collective-permute-start | bytes 1769480 | tf_op jit(solution)/shard_map/ppermute | solution.py:707
  332.8 18.2 %collective-permute-start.19 = (bf16[96,4736]{1,0:T(8,128)(2,1)}, bf16[96,4736]{1,0:T(8,128)(2,1)S(1)}, u32[]{:S(2)}, u32[]{:S(2)}) collective-permute-start(bf16[96,4736]{1,0:T(8,128)(2,1)} %get-tuple-element.246), channel_id=1, source_target_pairs={{0,8},{1,3},{2,10},{3,5},{4,12},{5,7},{6,14},{7,1},{8,16},{9,11},{... | collective-permute-start | bytes 2727944 | tf_op jit(solution)/shard_map/ppermute | solution.py:821
  333.4 17.6 %collective-permute-start.20 = (bf16[96,4736]{1,0:T(8,128)(2,1)}, bf16[96,4736]{1,0:T(8,128)(2,1)}, u32[]{:S(2)}, u32[]{:S(2)}) collective-permute-start(bf16[96,4736]{1,0:T(8,128)(2,1)} %get-tuple-element.247), channel_id=1, source_target_pairs={{0,24},{1,7},{2,26},{3,1},{4,28},{5,3},{6,30},{7,5},{8,0},{9,15},{... | collective-permute-start | bytes 2727944 | tf_op jit(solution)/shard_map/ppermute | solution.py:821
  348.0 14.2 %collective-permute-start.12 = (bf16[96,4736]{1,0:T(8,128)(2,1)}, bf16[96,4736]{1,0:T(8,128)(2,1)S(1)}, u32[]{:S(2)}, u32[]{:S(2)}) collective-permute-start(bf16[96,4736]{1,0:T(8,128)(2,1)} %get-tuple-element.235), channel_id=1, source_target_pairs={{0,8},{1,3},{2,10},{3,5},{4,12},{5,7},{6,14},{7,1},{8,16},{9,11},{... | collective-permute-start | bytes 2727944 | tf_op jit(solution)/shard_map/ppermute | solution.py:821
  348.3 13.8 %collective-permute-start.13 = (bf16[96,4736]{1,0:T(8,128)(2,1)}, bf16[96,4736]{1,0:T(8,128)(2,1)S(1)}, u32[]{:S(2)}, u32[]{:S(2)}) collective-permute-start(bf16[96,4736]{1,0:T(8,128)(2,1)} %get-tuple-element.236), channel_id=1, source_target_pairs={{0,24},{1,7},{2,26},{3,1},{4,28},{5,3},{6,30},{7,5},{8,0},{9,15},{... | collective-permute-start | bytes 2727944 | tf_op jit(solution)/shard_map/ppermute | solution.py:821
  354.7 27.0 %collective-permute-start.21 = (bf16[192,4736]{1,0:T(8,128)(2,1)S(1)}, bf16[192,4736]{1,0:T(8,128)(2,1)S(1)}, u32[]{:S(2)}, u32[]{:S(2)}) collective-permute-start(bf16[192,4736]{1,0:T(8,128)(2,1)S(1)} %get-tuple-element.248), channel_id=1, source_target_pairs={{0,8},{1,3},{2,10},{3,5},{4,12},{5,7},{6,14},{7,1},{8,16},{9,11},{... | collective-permute-start | bytes 5455880 | tf_op jit(solution)/shard_map/ppermute | solution.py:821
  354.7 28.2 %collective-permute-start.22 = (bf16[192,4736]{1,0:T(8,128)(2,1)S(1)}, bf16[192,4736]{1,0:T(8,128)(2,1)}, u32[]{:S(2)}, u32[]{:S(2)}) collective-permute-start(bf16[192,4736]{1,0:T(8,128)(2,1)S(1)} %get-tuple-element.249), channel_id=1, source_target_pairs={{0,24},{1,7},{2,26},{3,1},{4,28},{5,3},{6,30},{7,5},{8,0},{9,15},{... | collective-permute-start | bytes 5455880 | tf_op jit(solution)/shard_map/ppermute | solution.py:821
  364.7 46.3 %collective-permute-start.14 = (bf16[192,4736]{1,0:T(8,128)(2,1)S(1)}, bf16[192,4736]{1,0:T(8,128)(2,1)}, u32[]{:S(2)}, u32[]{:S(2)}) collective-permute-start(bf16[192,4736]{1,0:T(8,128)(2,1)S(1)} %get-tuple-element.237), channel_id=1, source_target_pairs={{0,8},{1,3},{2,10},{3,5},{4,12},{5,7},{6,14},{7,1},{8,16},{9,11},{... | collective-permute-start | bytes 5455880 | tf_op jit(solution)/shard_map/ppermute | solution.py:821
  364.7 46.2 %collective-permute-start.15 = (bf16[192,4736]{1,0:T(8,128)(2,1)S(1)}, bf16[192,4736]{1,0:T(8,128)(2,1)}, u32[]{:S(2)}, u32[]{:S(2)}) collective-permute-start(bf16[192,4736]{1,0:T(8,128)(2,1)S(1)} %get-tuple-element.238), channel_id=1, source_target_pairs={{0,24},{1,7},{2,26},{3,1},{4,28},{5,3},{6,30},{7,5},{8,0},{9,15},{... | collective-permute-start | bytes 5455880 | tf_op jit(solution)/shard_map/ppermute | solution.py:821
  387.4 31.9 %collective-permute-start.23 = (bf16[48,4736]{1,0:T(8,128)(2,1)}, bf16[48,4736]{1,0:T(8,128)(2,1)S(1)}, u32[]{:S(2)}, u32[]{:S(2)}) collective-permute-start(bf16[48,4736]{1,0:T(8,128)(2,1)} %get-tuple-element.251), channel_id=1, source_target_pairs={{0,2},{1,9},{2,4},{3,11},{4,6},{5,13},{6,0},{7,15},{8,10},{9,17},{... | collective-permute-start | bytes 1363976 | tf_op jit(solution)/shard_map/ppermute | solution.py:821
  388.4 31.8 %collective-permute-start.24 = (bf16[48,4736]{1,0:T(8,128)(2,1)}, bf16[48,4736]{1,0:T(8,128)(2,1)S(1)}, u32[]{:S(2)}, u32[]{:S(2)}) collective-permute-start(bf16[48,4736]{1,0:T(8,128)(2,1)} %get-tuple-element.252), channel_id=1, source_target_pairs={{0,4},{1,17},{2,6},{3,19},{4,0},{5,21},{6,2},{7,23},{8,12},{9,25},... | collective-permute-start | bytes 1363976 | tf_op jit(solution)/shard_map/ppermute | solution.py:821
  391.2 29.0 %collective-permute-start.25 = (bf16[48,4736]{1,0:T(8,128)(2,1)}, bf16[48,4736]{1,0:T(8,128)(2,1)S(1)}, u32[]{:S(2)}, u32[]{:S(2)}) collective-permute-start(bf16[48,4736]{1,0:T(8,128)(2,1)} %get-tuple-element.253), channel_id=1, source_target_pairs={{0,6},{1,25},{2,0},{3,27},{4,2},{5,29},{6,4},{7,31},{8,14},{9,1},{... | collective-permute-start | bytes 1363976 | tf_op jit(solution)/shard_map/ppermute | solution.py:821
  416.5 13.9 %collective-permute-start.17 = (bf16[48,4736]{1,0:T(8,128)(2,1)}, bf16[48,4736]{1,0:T(8,128)(2,1)S(1)}, u32[]{:S(2)}, u32[]{:S(2)}) collective-permute-start(bf16[48,4736]{1,0:T(8,128)(2,1)} %get-tuple-element.241), channel_id=1, source_target_pairs={{0,4},{1,17},{2,6},{3,19},{4,0},{5,21},{6,2},{7,23},{8,12},{9,25},... | collective-permute-start | bytes 1363976 | tf_op jit(solution)/shard_map/ppermute | solution.py:821
  419.3 11.2 %collective-permute-start.18 = (bf16[48,4736]{1,0:T(8,128)(2,1)}, bf16[48,4736]{1,0:T(8,128)(2,1)S(1)}, u32[]{:S(2)}, u32[]{:S(2)}) collective-permute-start(bf16[48,4736]{1,0:T(8,128)(2,1)} %get-tuple-element.242), channel_id=1, source_target_pairs={{0,6},{1,25},{2,0},{3,27},{4,2},{5,29},{6,4},{7,31},{8,14},{9,1},{... | collective-permute-start | bytes 1363976 | tf_op jit(solution)/shard_map/ppermute | solution.py:821
  434.5 9.4 %collective-permute-start.26 = (bf16[24,4736]{1,0:T(8,128)(2,1)S(1)}, bf16[24,4736]{1,0:T(8,128)(2,1)S(1)}, u32[]{:S(2)}, u32[]{:S(2)}) collective-permute-start(bf16[24,4736]{1,0:T(8,128)(2,1)S(1)} %get-tuple-element.255), channel_id=1, source_target_pairs={{0,32},{32,0},{64,96},{96,64},{1,33},{33,1},{65,97},{97,65},{2,34}... | collective-permute-start | bytes 681992 | tf_op jit(solution)/shard_map/ppermute | solution.py:707
  434.6 9.4 %collective-permute-start.27 = (bf16[24,4736]{1,0:T(8,128)(2,1)S(1)}, bf16[24,4736]{1,0:T(8,128)(2,1)S(1)}, u32[]{:S(2)}, u32[]{:S(2)}) collective-permute-start(bf16[24,4736]{1,0:T(8,128)(2,1)S(1)} %get-tuple-element.256), channel_id=1, source_target_pairs={{0,1},{1,0},{2,3},{3,2},{4,5},{5,4},{6,7},{7,6},{8,9},{9,8},{10,11... | collective-permute-start | bytes 681992 | tf_op jit(solution)/shard_map/ppermute | solution.py:703
  439.2 9.7 %collective-permute-start.28 = (bf16[24,4736]{1,0:T(8,128)(2,1)S(1)}, bf16[24,4736]{1,0:T(8,128)(2,1)S(1)}, u32[]{:S(2)}, u32[]{:S(2)}) collective-permute-start(bf16[24,4736]{1,0:T(8,128)(2,1)S(1)} %get-tuple-element.257), channel_id=1, source_target_pairs={{0,33},{1,32},{2,35},{3,34},{4,37},{5,36},{6,39},{7,38},{8,41},{9,... | collective-permute-start | bytes 681992 | tf_op jit(solution)/shard_map/ppermute | solution.py:914
  (26 other events, 189.2 us)
Sparse Core Ops, SparseCore 0:
  24.3 105.4 all-gather.2
